TPU v7x, 32 devices: a whole 2x2x4 slice. The times are simulated.
32 devices in a mesh: img: 8 (over z, y), seq: 4 (over x, core).
Axes of the slice: x: 2, y: 2, z: 4, core: 2. Of those that a mesh axis runs over, the one named last changes fastest.
Arguments:
- tokens: bfloat16 [8, 732, 1152], P('img', 'seq'), may hold values from -6 to 6
- offsets: int32 [8], P('img'), may hold values from 0 to 3
- w_qkv: bfloat16 [1152, 3456], P(('img', 'seq'))
- w_out: bfloat16 [1152, 1152], P(('img', 'seq')), may hold values from -4 to 4
- w_fc1: bfloat16 [1152, 4304], P(('img', 'seq')), may hold values from -0.1875 to 0.1875
- w_fc2: bfloat16 [1152, 4304], P(('img', 'seq')), may hold values from -0.09375 to 0.09375
- gains: bfloat16 [1152, 2], P(('img', 'seq')), may hold values from 0.25 to 1.75
- biases: bfloat16 [1152, 6], P(('img', 'seq')), may hold values from -3 to 3
- fc1_bias: bfloat16 [4304], replicated, may hold values from -3 to 3
- cotangent: bfloat16 [8, 732, 1152], P('img', 'seq'), may hold values from -6 to 6
Outputs:
- mixed: float32 [8, 732, 1152], P('img', 'seq')
- grad_tokens: float32 [8, 732, 1152], P('img', 'seq')
- grad_qkv: float32 [1152, 3456], P(('img', 'seq'))
- grad_out: float32 [1152, 1152], P(('img', 'seq'))
- grad_fc1: float32 [1152, 4304], P(('img', 'seq'))
- grad_fc2: float32 [1152, 4304], P(('img', 'seq'))
- grad_gains: float32 [1152, 2], P(('img', 'seq'))
- grad_biases: float32 [1152, 6], P(('img', 'seq'))
- grad_fc1_bias: float32 [4304], replicated
Inputs may be any that keep to these rules, and one draw needn't show every extreme that they name: Image i's real tokens are positions offsets[i] to offsets[i] + 728.
All inputs are finite; a program needn't handle non-finite values.
Results may differ from a plain program's by a relative error of at most 0.012.
Values may be sent and summed in bfloat16 or wider, within the bound.
A program may use at most 256 MiB of HBM per device.

v0:
```python
from functools import partial

import jax
import jax.numpy as jnp
from jax import lax
from jax.sharding import PartitionSpec as P

HEADS = 16
VALID = 729


masked_score = -1000000000.0
norm_epsilon = 1e-06


def layer_norm(values, gain_col, bias_col):
    average = jnp.mean(values, -1, keepdims=True)
    centered = values - average
    variance = jnp.mean(centered * centered, -1, keepdims=True)
    return centered * lax.rsqrt(variance + norm_epsilon) * gain_col + bias_col


def row_dot(left, right):
    return lax.dot_general(
        left, right, (((0,), (0,)), ((), ())), preferred_element_type=jnp.float32
    )


def last_dot(left, right):
    return lax.dot_general(
        left, right, (((1,), (1,)), ((), ())), preferred_element_type=jnp.float32
    )


def split_heads(tensor, images_here, count, head_count, head_dim):
    return tensor.reshape(images_here, count, head_count, head_dim).transpose(2, 0, 1, 3)


def join_heads(tensor):
    head_count, images_here, count, head_dim = tensor.shape
    return tensor.transpose(1, 2, 0, 3).reshape(images_here, count, head_count * head_dim)


def local(tokens, offsets, w_qkv, w_out, w_fc1, w_fc2, gains, biases, fc1_bias, cotangent):
    images_here, slice_len, model_width = tokens.shape
    head_count = HEADS
    head_dim = model_width // head_count
    length = slice_len * lax.axis_size("seq")
    row_count = images_here * slice_len
    score_scale = head_dim ** (-0.5)
    gathered = (
        lax.all_gather(w_qkv, ("img", "seq"), axis=0, tiled=True),
        lax.all_gather(w_out, ("img", "seq"), axis=0, tiled=True),
        lax.all_gather(w_fc1, ("img", "seq"), axis=0, tiled=True),
        lax.all_gather(w_fc2, ("img", "seq"), axis=0, tiled=True),
        lax.all_gather(gains, ("img", "seq"), axis=0, tiled=True),
        lax.all_gather(biases, ("img", "seq"), axis=0, tiled=True),
    )
    wide_qkv, wide_out, wide_fc1, wide_fc2, gain_all, bias_all = gathered
    gain_cols = gain_all.astype(jnp.float32)
    bias_cols = bias_all.astype(jnp.float32)
    starts = offsets[:, None]
    positions = lax.axis_index("seq") * slice_len + jnp.arange(slice_len, dtype=jnp.int32)
    own_valid = (positions[None, :] >= starts) & (positions[None, :] < starts + VALID)
    row_valid = own_valid.astype(jnp.float32)
    key_pos = jnp.arange(length, dtype=jnp.int32)
    key_valid = (key_pos[None, :] >= starts) & (key_pos[None, :] < starts + VALID)
    inputs = tokens.astype(jnp.float32).reshape(row_count, model_width)
    h_one, norm_one_back = jax.vjp(layer_norm, inputs, gain_cols[:, 0], bias_cols[:, 0])
    h_one_low = h_one.astype(jnp.bfloat16)
    qkv_bias = jnp.concatenate([bias_cols[:, 1], jnp.zeros_like(bias_cols[:, 1]), bias_cols[:, 2]])
    projected = (
        jnp.dot(h_one_low, wide_qkv, preferred_element_type=jnp.float32) + qkv_bias
    ).astype(jnp.bfloat16)
    query_rows = projected[:, :model_width]
    key_rows = projected[:, model_width : 2 * model_width].reshape(
        images_here, slice_len, model_width
    )
    value_rows = projected[:, 2 * model_width :].reshape(images_here, slice_len, model_width)
    keys_all, values_all = (
        lax.all_gather(key_rows, "seq", axis=1, tiled=True),
        lax.all_gather(value_rows, "seq", axis=1, tiled=True),
    )
    query_heads = split_heads(query_rows, images_here, slice_len, head_count, head_dim)
    key_heads = split_heads(keys_all, images_here, length, head_count, head_dim)
    value_heads = split_heads(values_all, images_here, length, head_count, head_dim)

    def head_scores(head_query_rows, head_key_rows, mask):
        scores = (
            jnp.einsum(
                "asl,aul->asu", head_query_rows, head_key_rows, preferred_element_type=jnp.float32
            )
            * score_scale
        )
        return jnp.where(mask[:, None, :], scores, masked_score)

    def forward_head(head_args):
        head_query_rows, head_key_rows, head_value_rows = head_args
        scores = head_scores(head_query_rows, head_key_rows, key_valid)
        maxima = jnp.max(scores, -1, keepdims=True)
        exponent = jnp.exp(scores - maxima)
        totals_row = jnp.sum(exponent, -1, keepdims=True)
        probs = exponent / totals_row
        attended_head = jnp.einsum(
            "owz,ozf->owf",
            probs.astype(jnp.bfloat16),
            head_value_rows,
            preferred_element_type=jnp.float32,
        )
        return (attended_head, maxima[..., 0] + jnp.log(totals_row[..., 0]))

    attended_heads, log_total = lax.map(forward_head, (query_heads, key_heads, value_heads))
    attended = join_heads(attended_heads).reshape(row_count, model_width).astype(jnp.bfloat16)
    middle = (
        inputs + jnp.dot(attended, wide_out, preferred_element_type=jnp.float32) + bias_cols[:, 3]
    )
    h_two, norm_two_back = jax.vjp(layer_norm, middle, gain_cols[:, 1], bias_cols[:, 4])
    h_two_low = h_two.astype(jnp.bfloat16)
    preact = jnp.dot(h_two_low, wide_fc1, preferred_element_type=jnp.float32) + fc1_bias.astype(
        jnp.float32
    )
    activated, gelu_back = jax.vjp(partial(jax.nn.gelu, approximate=True), preact)
    activated_low = activated.astype(jnp.bfloat16)
    branch_two = last_dot(activated_low, wide_fc2) + bias_cols[:, 5]
    valid_rows = row_valid.reshape(row_count, 1)
    mixed = (valid_rows * (middle + branch_two)).reshape(images_here, slice_len, model_width)
    wide_qkv, wide_out, wide_fc1, wide_fc2 = (
        lax.all_gather(w_qkv, ("img", "seq"), axis=0, tiled=True),
        lax.all_gather(w_out, ("img", "seq"), axis=0, tiled=True),
        lax.all_gather(w_fc1, ("img", "seq"), axis=0, tiled=True),
        lax.all_gather(w_fc2, ("img", "seq"), axis=0, tiled=True),
    )
    grad_output = cotangent.astype(jnp.float32).reshape(row_count, model_width) * valid_rows
    grad_branch = grad_output.astype(jnp.bfloat16)
    grad_bias_two = jnp.sum(grad_branch.astype(jnp.float32), 0)
    grad_fc2_local = row_dot(grad_branch, activated_low)
    grad_activated = jnp.dot(grad_branch, wide_fc2, preferred_element_type=jnp.float32)
    (grad_preact,) = gelu_back(grad_activated)
    preact_low = grad_preact.astype(jnp.bfloat16)
    grad_hidden_bias = jnp.sum(preact_low.astype(jnp.float32), 0)
    grad_fc1_local = row_dot(h_two_low, preact_low)
    grad_h_two = last_dot(preact_low, wide_fc1)
    grad_middle_norm, grad_gain_two, grad_shift_two = norm_two_back(grad_h_two)
    grad_middle = grad_output + grad_middle_norm
    grad_branch_one = grad_middle.astype(jnp.bfloat16)
    grad_out_bias = jnp.sum(grad_branch_one.astype(jnp.float32), 0)
    output_gradient_shard = row_dot(attended, grad_branch_one)
    grad_attended = last_dot(grad_branch_one, wide_out).astype(jnp.bfloat16)
    grad_att_heads = split_heads(grad_attended, images_here, slice_len, head_count, head_dim)

    def backward_head(head_args):
        head_query_rows, head_key_rows, head_value_rows, head_gradient, total_head = head_args
        scores = head_scores(head_query_rows, head_key_rows, key_valid)
        probs = jnp.exp(scores - total_head[..., None])
        grad_probs = jnp.einsum(
            "asl,aul->asu", head_gradient, head_value_rows, preferred_element_type=jnp.float32
        )
        grad_scores = probs * (grad_probs - jnp.sum(probs * grad_probs, -1, keepdims=True))
        reduced_scores = grad_scores.astype(jnp.bfloat16)
        grad_query = (
            jnp.einsum(
                "owz,ozf->owf", reduced_scores, head_key_rows, preferred_element_type=jnp.float32
            )
            * score_scale
        )
        grad_key = (
            jnp.einsum(
                "xzl,xzv->xlv", reduced_scores, head_query_rows, preferred_element_type=jnp.float32
            )
            * score_scale
        )
        grad_value = jnp.einsum(
            "xzl,xzv->xlv",
            probs.astype(jnp.bfloat16),
            head_gradient,
            preferred_element_type=jnp.float32,
        )
        return (grad_query, grad_key, grad_value)

    grad_q_heads, grad_k_heads, grad_v_heads = lax.map(
        backward_head, (query_heads, key_heads, value_heads, grad_att_heads, log_total)
    )
    key_gradient_rows, grad_values = (
        lax.psum_scatter(
            join_heads(grad_k_heads).astype(jnp.bfloat16), "seq", scatter_dimension=1, tiled=True
        ).astype(jnp.float32),
        lax.psum_scatter(
            join_heads(grad_v_heads).astype(jnp.bfloat16), "seq", scatter_dimension=1, tiled=True
        ).astype(jnp.float32),
    )
    grad_projected = jnp.concatenate(
        [
            join_heads(grad_q_heads).reshape(row_count, model_width),
            key_gradient_rows.reshape(row_count, model_width),
            grad_values.reshape(row_count, model_width),
        ],
        1,
    ).astype(jnp.bfloat16)
    grad_query_bias = jnp.sum(grad_projected[:, :model_width].astype(jnp.float32), 0)
    grad_value_bias = jnp.sum(grad_projected[:, 2 * model_width :].astype(jnp.float32), 0)
    grad_qkv_local = row_dot(h_one_low, grad_projected)
    grad_h_one = last_dot(grad_projected, wide_qkv)
    grad_input_norm, grad_gain_one, grad_shift_one = norm_one_back(grad_h_one)
    grad_tokens = (grad_middle + grad_input_norm).reshape(images_here, slice_len, model_width)
    grad_gain_local = jnp.stack([grad_gain_one, grad_gain_two], 1)
    grad_bias_local = jnp.stack(
        [
            grad_shift_one,
            grad_query_bias,
            grad_value_bias,
            grad_out_bias,
            grad_shift_two,
            grad_bias_two,
        ],
        1,
    )
    owned = (
        lax.psum_scatter(grad_qkv_local, ("img", "seq"), scatter_dimension=0, tiled=True),
        lax.psum_scatter(output_gradient_shard, ("img", "seq"), scatter_dimension=0, tiled=True),
        lax.psum_scatter(grad_fc1_local, ("img", "seq"), scatter_dimension=0, tiled=True),
        lax.psum_scatter(grad_fc2_local, ("img", "seq"), scatter_dimension=0, tiled=True),
        lax.psum_scatter(grad_gain_local, ("img", "seq"), scatter_dimension=0, tiled=True),
        lax.psum_scatter(grad_bias_local, ("img", "seq"), scatter_dimension=0, tiled=True),
    )
    hidden_bias_total = lax.psum(grad_hidden_bias, ("img", "seq"))
    return (
        mixed,
        grad_tokens,
        owned[0],
        owned[1],
        owned[2],
        owned[3],
        owned[4],
        owned[5],
        hidden_bias_total,
    )


def solution(mesh):
    in_specs = (
        P("img", "seq", None),
        P("img"),
        P(("img", "seq"), None),
        P(("img", "seq"), None),
        P(("img", "seq"), None),
        P(("img", "seq"), None),
        P(("img", "seq"), None),
        P(("img", "seq"), None),
        P(),
        P("img", "seq", None),
    )
    out_specs = (
        P("img", "seq", None),
        P("img", "seq", None),
        P(("img", "seq"), None),
        P(("img", "seq"), None),
        P(("img", "seq"), None),
        P(("img", "seq"), None),
        P(("img", "seq"), None),
        P(("img", "seq"), None),
        P(),
    )
    return jax.shard_map(local, mesh=mesh, in_specs=in_specs, out_specs=out_specs, check_vma=False)
```

profile of v0, /device:TPU:1, one launch (start us, length us, event | category | flops | bytes accessed | tf_op | source)
XLA Modules:
  0.0 1646.3 jit_solution(13942547134678637957)
XLA Ops:
  8.7 43.1 %all-gather.2 = bf16[32,36,2]{1,2,0:T(2,128)(2,1)S(1)} all-gather(bf16[1,36,2]{1,2,0:T(2,128)(2,1)} %bitcast.240), channel_id=1, replica_groups=mesh['img'=8,'seq'=4] {'img','seq'}, dimensions={0}, use_global_device_ids=true | all-gather | bytes 4752 | tf_op jit(solution)/shard_map/all_gather | solution.py:56
  51.9 37.9 %all-gather.3 = bf16[32,36,6]{1,2,0:T(8,128)(2,1)S(1)} all-gather(bf16[1,36,6]{1,2,0:T(8,128)(2,1)} %bitcast.239), channel_id=1, replica_groups=mesh['img'=8,'seq'=4] {'img','seq'}, dimensions={0}, use_global_device_ids=true | all-gather | bytes 14256 | tf_op jit(solution)/shard_map/all_gather | solution.py:57
  93.1 12.5 reshape.346
  105.6 5.3 fusion.50
  116.4 37.2 %all-gather.23.cloned.1.call-done = bf16[32,36,1152]{2,1,0:T(8,128)(2,1)} async-done(((bf16[1,36,1152]{2,1,0:T(8,128)(2,1)}), bf16[32,36,1152]{2,1,0:T(8,128)(2,1)}) %all-gather.23.cloned.1.call-update) | async-done | bytes 2654224 | tf_op jit(solution)/shard_map/all_gather | solution.py:53
  153.7 3.6 reshape.352
  159.7 15.2 all-gather.19.cloned.1.call-done
  174.9 4.9 copy.58
  179.8 5.2 reshape.325
  185.0 12.3 all-gather.21.cloned.1.call-done
  197.3 4.9 copy.59
  202.2 5.2 reshape.327
  207.4 4.4 copy.62
  211.7 4.4 copy.61
  216.1 65.9 %while.28 = (s32[]{:T(128)}, bf16[16,1,183,72]{2,3,1,0:T(8,128)(2,1)S(1)}, f32[16,1,183]{2,1,0:T(1,128)}, bf16[16,1,183,72]{3,2,1,0:T(8,128)(2,1)}, bf16[16,1,73...) while((s32[]{:T(128)}, ...), condition=%wide.region_5.6_spmd.clone, body=%wide.region_2.5_spmd.clone.sunk | while | flops 39652988 | bytes 2146381 | solution.py:112
  285.3 4.2 all-gather.25.cloned.1.call-done
  289.5 14.5 reshape.354
  304.0 6.3 convolution_add_fusion
  311.9 8.8 fusion.83
  320.8 259.4 %fusion.7 = f32[40,4304]{1,0:T(8,128)} fusion(f32[1152,4304]{1,0:T(8,128)} %fusion.83), kind=kCustom, calls=%all-reduce-scatter.3 | all-reduce-scatter fusion | flops 5509121 | bytes 20521472
  580.2 5.8 collective-permute-start.22
  586.0 5.8 collective-permute-start.21
  593.9 14.4 reshape.356
  608.4 10.0 convert_reduce_fusion
  618.4 8.4 fusion.61
  626.9 5.6 multiply_reduce_fusion.1
  638.0 124.6 %while.29 = (s32[]{:T(128)}, bf16[16,1,183,72]{2,3,1,0:T(8,128)(2,1)S(1)}, bf16[16,1,732,72]{2,3,1,0:T(8,128)(2,1)}, bf16[16,1,732,72]{2,3,1,0:T(8,128)(2,1)}, b...) while((s32[]{:T(128)}, ...), condition=%wide.region_12.13_spmd.clone, body=%wide.region_10.12_spmd.clone.sunk | while | flops 97721808 | bytes 5322477 | solution.py:180
  762.7 11.9 fusion.92
  776.2 3.3 fusion.99
  784.5 17.5 %concatenate.12 = f32[164,4304]{1,0:T(8,128)} concatenate(f32[4,4304]{1,0:T(4,128)S(1)} %collective-permute-done.23, f32[40,4304]{1,0:T(8,128)} %collective-permute-done.22, f32[40,4304]{1,0:T(8,128)} %collective-permute-done.21, f32[40,4304]{1,0:T(8,128)} %collective-permute-done.20, f32[40,4304]{1,0:T(8,128)S(1)} %copy-done.14), dimensions={0} | concatenate | bytes 5646848
  804.2 33.9 %all-reduce.17.cloned.1.call-done = (bf16[1,732,1152]{1,2,0:T(8,128)(2,1)}, bf16[1,732,1152]{1,2,0:T(8,128)(2,1)}) async-done(((bf16[1,732,1152]{1,2,0:T(8,128)(2,1)}, bf16[1,732,1152]{1,2,0:T(8,128)(2,1)}), (bf16[1,732,1152]{1,2,0:T(8,128)(2,1)}, bf16[1,732,1152]{1,2,0:T(8,128)(2,1)})) %all-reduce.17.cloned.1.call-update) | async-done | bytes 3373072
  841.8 8.1 fusion.76
  850.0 530.5 %fusion.94 = (f32[48,3456]{1,0:T(8,128)S(1)}, f32[48,1152]{1,0:T(8,128)}, f32[40,4304]{1,0:T(8,128)S(1)}) fusion(f32[1152,3456]{1,0:T(8,128)} %fusion.76, f32[1152,1152]{1,0:T(8,128)} %fusion.99, f32[1152,4304]{1,0:T(8,128)} %fusion.92), kind=kCustom, calls=%all-reduce-scatter.4 | all-reduce-scatter fusion | flops 12587010 | bytes 42639872
  1383.8 3.1 collective-permute-start.15
  1386.9 6.4 fusion.93
  1393.2 14.3 collective-permute-start.13
  1410.3 5.8 collective-permute-start.10
  1418.6 2.5 collective-permute-start.9
  1421.1 3.3 collective-permute-start.8
  1425.9 7.7 collective-permute-start.5
  1433.6 12.2 collective-permute-start.4
  1448.9 8.5 collective-permute-start.2
  1464.4 89.7 %all-reduce.12 = (f32[1152,2]{0,1:T(2,128)S(1)}, f32[1152,6]{0,1:T(8,128)S(1)}, f32[4304]{0:T(1024)}) all-reduce(f32[1152,2]{0,1:T(2,128)S(1)} %pad_maximum_fusion.4, f32[1152,6]{0,1:T(8,128)S(1)} %stack.39, f32[4304]{0:T(1024)S(1)} %copy-done.39), channel_id=10, replica_groups=mesh['img'=8,'seq'=4] {'img','seq'}, use_global_device_ids=true, to_apply=%region_23.24.clone | all-reduce | flops 13520 | bytes 108160
  1555.4 14.4 concatenate.10
  1569.8 4.1 collective-permute-start.18
  1574.0 4.2 collective-permute-start.17
  1584.2 36.8 %concatenate.9 = f32[420,3456]{1,0:T(8,128)} concatenate(f32[36,3456]{1,0:T(8,128)} %copy-done.20, f32[48,3456]{1,0:T(8,128)} %copy-done.19, f32[48,3456]{1,0:T(8,128)} %collective-permute-done.5, f32[48,3456]{1,0:T(8,128)} %collective-permute-done.4, f32[48,3456]{1,0:T(8,128)} %collective-permute-done.3, f32[48,3456]{1,0:T(8,128)} %collective-permute-done.2, ...), dimensions={0} | concatenate | bytes 11612160
  1623.7 14.5 concatenate.11
  (452 shorter events, 256.3 us)
Async XLA Ops:
  7.2 86.0 %all-gather.17.cloned.1.call-start = ((), (), s32[]{:S(2)}) async-start(), calls=%async_computation | async-start | bytes 9123840 | tf_op jit(solution)/shard_map/all_gather | solution.py:52
  7.9 145.8 %all-gather.23.cloned.1.call-start = ((), (), s32[]{:S(2)}) async-start(), calls=%async_computation.3 | async-start | bytes 3041280 | tf_op jit(solution)/shard_map/all_gather | solution.py:53
  8.7 166.2 %all-gather.19.cloned.1.call-start = ((), (), s32[]{:S(2)}) async-start(), calls=%async_computation.1 | async-start | bytes 2119680 | tf_op jit(solution)/shard_map/all_gather | solution.py:81
  112.1 85.2 %all-gather.21.cloned.1.call-start = ((), (), s32[]{:S(2)}) async-start(), calls=%async_computation.2 | async-start | bytes 2119680 | tf_op jit(solution)/shard_map/all_gather | solution.py:82
  112.6 176.8 %all-gather.25.cloned.1.call-start = ((), (), s32[]{:S(2)}) async-start(), calls=%async_computation.4 | async-start | bytes 11489280 | tf_op jit(solution)/shard_map/all_gather | solution.py:54
  113.2 480.7 %all-gather.27.cloned.1.call-start = ((), (), s32[]{:S(2)}) async-start(), calls=%async_computation.5 | async-start | bytes 11489280 | tf_op jit(solution)/shard_map/all_gather | solution.py:55
  113.8 724.3 %all-reduce.17.cloned.1.call-start = ((), (), s32[]{:S(2)}) async-start(), calls=%async_computation.6 | async-start | bytes 7077888
  116.4 516.5 %copy-start.30 = (f32[183]{0:T(256)}, f32[183]{0:T(256)S(1)}, u32[]{:S(2)}) copy-start(f32[183]{0:T(256)S(1)} %and_convert_fusion) | copy-start | bytes 2200
  580.2 204.3 %collective-permute-start.22 = (f32[40,4304]{1,0:T(8,128)}, f32[40,4304]{1,0:T(8,128)}, u32[]{:S(2)}, u32[]{:S(2)}) collective-permute-start(f32[40,4304]{1,0:T(8,128)} %fusion.7), channel_id=1, source_target_pairs={{0,3},{1,4},{2,5},{3,6},{4,7},{5,8},{6,9},{7,10},{8,11},{9,12},{10... | collective-permute-start | bytes 2065928
  586.0 198.6 %collective-permute-start.21 = (f32[40,4304]{1,0:T(8,128)}, f32[40,4304]{1,0:T(8,128)}, u32[]{:S(2)}, u32[]{:S(2)}) collective-permute-start(f32[40,4304]{1,0:T(8,128)} %fusion.7), channel_id=1, source_target_pairs={{0,2},{1,3},{2,4},{3,5},{4,6},{5,7},{6,8},{7,9},{8,10},{9,11},{10,... | collective-permute-start | bytes 2065928
  591.8 192.7 %collective-permute-start.20 = (f32[40,4304]{1,0:T(8,128)}, f32[40,4304]{1,0:T(8,128)}, u32[]{:S(2)}, u32[]{:S(2)}) collective-permute-start(f32[40,4304]{1,0:T(8,128)} %fusion.7), channel_id=1, source_target_pairs={{0,1},{1,2},{2,3},{3,4},{4,5},{5,6},{6,7},{7,8},{8,9},{9,10},{10,1... | collective-permute-start | bytes 2065928
  774.7 9.8 collective-permute-start.23
  802.1 39.7 %copy-start.33 = (f32[183]{0:T(256)S(1)}, f32[183]{0:T(256)}, u32[]{:S(2)}) copy-start(f32[183]{0:T(256)} %copy-done.32) | copy-start | bytes 2200
  802.1 39.8 %copy-start.36 = (f32[183]{0:T(256)S(1)}, f32[183]{0:T(256)}, u32[]{:S(2)}) copy-start(f32[183]{0:T(256)} %copy-done.35) | copy-start | bytes 2200
  1380.4 197.8 %copy-start.13 = (f32[40,4304]{1,0:T(8,128)}, f32[40,4304]{1,0:T(8,128)S(1)}, u32[]{:S(2)}) copy-start(f32[40,4304]{1,0:T(8,128)S(1)} %get-tuple-element.308) | copy-start | bytes 2065924
  1381.6 75.8 %copy-start.7 = (f32[183,1152]{1,0:T(8,128)S(1)}, f32[183,1152]{1,0:T(8,128)}, u32[]{:S(2)}) copy-start(f32[183,1152]{1,0:T(8,128)} %copy-done.6) | copy-start | bytes 2529796
  1381.6 75.8 %copy-start.10 = (bf16[1,183,1152]{2,1,0:T(8,128)(2,1)S(1)}, bf16[1,183,1152]{2,1,0:T(8,128)(2,1)}, u32[]{:S(2)}) copy-start(bf16[1,183,1152]{2,1,0:T(8,128)(2,1)} %param.23) | copy-start | bytes 1264900
  1381.7 75.7 %copy-start.31 = (f32[183]{0:T(256)S(1)}, f32[183]{0:T(256)}, u32[]{:S(2)}) copy-start(f32[183]{0:T(256)} %copy-done.30) | copy-start | bytes 2200
  1381.7 75.7 %copy-start.49 = (f32[183]{0:T(256)S(1)}, f32[183]{0:T(256)}, u32[]{:S(2)}) copy-start(f32[183]{0:T(256)} %copy-done.48) | copy-start | bytes 2200
  1381.7 34.4 %collective-permute-start.14 = (f32[48,1152]{1,0:T(8,128)}, f32[48,1152]{1,0:T(8,128)}, u32[]{:S(2)}, u32[]{:S(2)}) collective-permute-start(f32[48,1152]{1,0:T(8,128)} %get-tuple-element.307), channel_id=1, source_target_pairs={{0,7},{1,8},{2,9},{3,10},{4,11},{5,12},{6,13},{7,14},{8,15},{9,16}... | collective-permute-start | bytes 663560
  1383.8 26.5 %collective-permute-start.15 = (f32[36,1152]{1,0:T(8,128)S(1)}, f32[36,1152]{1,0:T(8,128)S(1)}, u32[]{:S(2)}, u32[]{:S(2)}) collective-permute-start(f32[36,1152]{1,0:T(8,128)S(1)} %slice.58), channel_id=1, source_target_pairs={{0,8},{1,9},{2,10},{3,11},{4,12},{5,13},{6,14},{7,15},{8,16},{9,17... | collective-permute-start | bytes 497672
  1393.2 64.6 %copy-start.38 = (f32[1152]{0:T(1024)S(1)}, f32[1152]{0:T(1024)}, u32[]{:S(2)}) copy-start(f32[1152]{0:T(1024)} %get-tuple-element.311) | copy-start | bytes 13828
  1393.2 25.4 %collective-permute-start.13 = (f32[48,1152]{1,0:T(8,128)S(1)}, f32[48,1152]{1,0:T(8,128)S(1)}, u32[]{:S(2)}, u32[]{:S(2)}) collective-permute-start(f32[48,1152]{1,0:T(8,128)S(1)} %copy-done.15), channel_id=1, source_target_pairs={{0,6},{1,7},{2,8},{3,9},{4,10},{5,11},{6,12},{7,13},{8,14},{9,15},... | collective-permute-start | bytes 663560
  1407.6 13.6 collective-permute-start.12
  1408.9 15.6 collective-permute-start.11
  1410.3 15.6 collective-permute-start.10
  1416.1 32.0 %collective-permute-start.7 = (f32[36,3456]{1,0:T(8,128)S(1)}, f32[36,3456]{1,0:T(8,128)S(1)}, u32[]{:S(2)}, u32[]{:S(2)}) collective-permute-start(f32[36,3456]{1,0:T(8,128)S(1)} %slice.57), channel_id=1, source_target_pairs={{0,8},{1,9},{2,10},{3,11},{4,12},{5,13},{6,14},{7,15},{8,16},{9,17... | collective-permute-start | bytes 1493000
  1418.1 41.6 %copy-start.40 = (f32[1152,1]{0,1:T(1,128)S(1)}, f32[1152,1]{0,1:T(1,128)}, u32[]{:S(2)}) copy-start(f32[1152,1]{0,1:T(1,128)} %stack.37) | copy-start | bytes 13828
  1418.1 41.6 %copy-start.41 = (f32[1152,1]{0,1:T(1,128)S(1)}, f32[1152,1]{0,1:T(1,128)}, u32[]{:S(2)}) copy-start(f32[1152,1]{0,1:T(1,128)} %stack.36) | copy-start | bytes 13828
  1418.1 41.6 %copy-start.42 = (f32[1152,1]{0,1:T(1,128)S(1)}, f32[1152,1]{0,1:T(1,128)}, u32[]{:S(2)}) copy-start(f32[1152,1]{0,1:T(1,128)} %stack.38) | copy-start | bytes 13828
  1418.1 41.6 %copy-start.43 = (f32[1152,1]{0,1:T(1,128)S(1)}, f32[1152,1]{0,1:T(1,128)}, u32[]{:S(2)}) copy-start(f32[1152,1]{0,1:T(1,128)} %stack.34) | copy-start | bytes 13828
  1418.1 46.2 %copy-start.44 = (f32[1152,1]{0,1:T(1,128)S(1)}, f32[1152,1]{0,1:T(1,128)}, u32[]{:S(2)}) copy-start(f32[1152,1]{0,1:T(1,128)} %stack.31) | copy-start | bytes 13828
  1418.1 46.2 %copy-start.39 = (f32[4304]{0:T(1024)S(1)}, f32[4304]{0:T(1024)}, u32[]{:S(2)}) copy-start(f32[4304]{0:T(1024)} %get-tuple-element.327) | copy-start | bytes 51652
  1418.2 137.2 %copy-start.16 = (f32[48,1152]{1,0:T(8,128)S(1)}, f32[48,1152]{1,0:T(8,128)}, u32[]{:S(2)}) copy-start(f32[48,1152]{1,0:T(8,128)} %get-tuple-element.307) | copy-start | bytes 663556
  1418.6 15.0 collective-permute-start.9
  1421.1 24.7 %collective-permute-start.8 = (f32[48,1152]{1,0:T(8,128)S(1)}, f32[48,1152]{1,0:T(8,128)S(1)}, u32[]{:S(2)}, u32[]{:S(2)}) collective-permute-start(f32[48,1152]{1,0:T(8,128)S(1)} %copy-done.15), channel_id=1, source_target_pairs={{0,1},{1,2},{2,3},{3,4},{4,5},{5,6},{6,7},{7,8},{8,9},{9,10},{10,1... | collective-permute-start | bytes 663560
  1424.5 35.3 %collective-permute-start.6 = (f32[48,3456]{1,0:T(8,128)S(1)}, f32[48,3456]{1,0:T(8,128)S(1)}, u32[]{:S(2)}, u32[]{:S(2)}) collective-permute-start(f32[48,3456]{1,0:T(8,128)S(1)} %get-tuple-element.306), channel_id=1, source_target_pairs={{0,7},{1,8},{2,9},{3,10},{4,11},{5,12},{6,13},{7,14},{8,15},{9,16}... | collective-permute-start | bytes 1990664
  1425.9 36.1 %collective-permute-start.5 = (f32[48,3456]{1,0:T(8,128)S(1)}, f32[48,3456]{1,0:T(8,128)}, u32[]{:S(2)}, u32[]{:S(2)}) collective-permute-start(f32[48,3456]{1,0:T(8,128)S(1)} %get-tuple-element.306), channel_id=1, source_target_pairs={{0,6},{1,7},{2,8},{3,9},{4,10},{5,11},{6,12},{7,13},{8,14},{9,15},... | collective-permute-start | bytes 1990664
  1433.6 136.2 %collective-permute-start.4 = (f32[48,3456]{1,0:T(8,128)S(1)}, f32[48,3456]{1,0:T(8,128)}, u32[]{:S(2)}, u32[]{:S(2)}) collective-permute-start(f32[48,3456]{1,0:T(8,128)S(1)} %get-tuple-element.306), channel_id=1, source_target_pairs={{0,5},{1,6},{2,7},{3,8},{4,9},{5,10},{6,11},{7,12},{8,13},{9,14},{... | collective-permute-start | bytes 1990664
  1445.9 128.1 %collective-permute-start.3 = (f32[48,3456]{1,0:T(8,128)S(1)}, f32[48,3456]{1,0:T(8,128)}, u32[]{:S(2)}, u32[]{:S(2)}) collective-permute-start(f32[48,3456]{1,0:T(8,128)S(1)} %get-tuple-element.306), channel_id=1, source_target_pairs={{0,4},{1,5},{2,6},{3,7},{4,8},{5,9},{6,10},{7,11},{8,12},{9,13},{1... | collective-permute-start | bytes 1990664
  1448.9 129.3 %collective-permute-start.2 = (f32[48,3456]{1,0:T(8,128)S(1)}, f32[48,3456]{1,0:T(8,128)}, u32[]{:S(2)}, u32[]{:S(2)}) collective-permute-start(f32[48,3456]{1,0:T(8,128)S(1)} %get-tuple-element.306), channel_id=1, source_target_pairs={{0,3},{1,4},{2,5},{3,6},{4,7},{5,8},{6,9},{7,10},{8,11},{9,12},{10... | collective-permute-start | bytes 1990664
  1459.8 110.0 %copy-start.19 = (f32[48,3456]{1,0:T(8,128)}, f32[48,3456]{1,0:T(8,128)S(1)}, u32[]{:S(2)}) copy-start(f32[48,3456]{1,0:T(8,128)S(1)} %collective-permute-done.6) | copy-start | bytes 1990660
  1459.8 121.9 %collective-permute-start.1 = (f32[48,3456]{1,0:T(8,128)S(1)}, f32[48,3456]{1,0:T(8,128)}, u32[]{:S(2)}, u32[]{:S(2)}) collective-permute-start(f32[48,3456]{1,0:T(8,128)S(1)} %get-tuple-element.306), channel_id=1, source_target_pairs={{0,2},{1,3},{2,4},{3,5},{4,6},{5,7},{6,8},{7,9},{8,10},{9,11},{10,... | collective-permute-start | bytes 1990664
  1462.0 122.2 %collective-permute-start = (f32[48,3456]{1,0:T(8,128)S(1)}, f32[48,3456]{1,0:T(8,128)}, u32[]{:S(2)}, u32[]{:S(2)}) collective-permute-start(f32[48,3456]{1,0:T(8,128)S(1)} %get-tuple-element.306), channel_id=1, source_target_pairs={{0,1},{1,2},{2,3},{3,4},{4,5},{5,6},{6,7},{7,8},{8,9},{9,10},{10,1... | collective-permute-start | bytes 1990664
  1569.8 53.0 %collective-permute-start.18 = (f32[40,4304]{1,0:T(8,128)S(1)}, f32[40,4304]{1,0:T(8,128)S(1)}, u32[]{:S(2)}, u32[]{:S(2)}) collective-permute-start(f32[40,4304]{1,0:T(8,128)S(1)} %get-tuple-element.308), channel_id=1, source_target_pairs={{0,3},{1,4},{2,5},{3,6},{4,7},{5,8},{6,9},{7,10},{8,11},{9,12},{10... | collective-permute-start | bytes 2065928
  1574.0 48.9 %collective-permute-start.17 = (f32[40,4304]{1,0:T(8,128)S(1)}, f32[40,4304]{1,0:T(8,128)}, u32[]{:S(2)}, u32[]{:S(2)}) collective-permute-start(f32[40,4304]{1,0:T(8,128)S(1)} %get-tuple-element.308), channel_id=1, source_target_pairs={{0,2},{1,3},{2,4},{3,5},{4,6},{5,7},{6,8},{7,9},{8,10},{9,11},{10,... | collective-permute-start | bytes 2065928
  1578.2 45.5 %collective-permute-start.16 = (f32[40,4304]{1,0:T(8,128)S(1)}, f32[40,4304]{1,0:T(8,128)}, u32[]{:S(2)}, u32[]{:S(2)}) collective-permute-start(f32[40,4304]{1,0:T(8,128)S(1)} %get-tuple-element.308), channel_id=1, source_target_pairs={{0,1},{1,2},{2,3},{3,4},{4,5},{5,6},{6,7},{7,8},{8,9},{9,10},{10,1... | collective-permute-start | bytes 2065928
  1581.8 41.1 %collective-permute-start.19 = (f32[4,4304]{1,0:T(4,128)S(1)}, f32[4,4304]{1,0:T(4,128)S(1)}, u32[]{:S(2)}, u32[]{:S(2)}) collective-permute-start(f32[4,4304]{1,0:T(4,128)S(1)} %slice.59), channel_id=1, source_target_pairs={{0,4},{1,5},{2,6},{3,7},{4,8},{5,9},{6,10},{7,11},{8,12},{9,13},{1... | collective-permute-start | bytes 206600
  (40 other events, 595.9 us)
Sparse Core Ops, SparseCore 0:
  10.9 82.1 all-gather.16
  96.1 57.5 all-gather.22
  155.8 19.0 all-gather.18
  176.9 20.3 all-gather.20
  200.0 89.4 all-gather.24
  292.2 129.4 all-gather.26
  762.8 75.2 all-reduce.16
where the time goes:
time: 1660 us; the launch traced here: 1650 us
  blocking collectives  961 us (58%)
  matrix products  220 us (13%)
  local copies, waits for them, and re-layouts  207 us (12%)
  waiting for transfers between devices  106 us (6%)
  starting transfers between devices  101 us (6%)
  other arithmetic  34.8 us (2%)
  between operations  16.8 us (1%)
    unnamed x3, blocking collectives  880 us
    unnamed x139, local copies, waits for them, and re-layouts  158 us
    unnamed x25, starting transfers between devices  101 us
    all_gather x1, blocking collectives, local(): lax.all_gather(gains, ('img', 'seq'), axis=0, tiled=True)  43.1 us
    dot_general x32, matrix products, head_scores(): jnp.einsum('asl,aul->asu', head_query_rows, head_key_rows, preferred_elem...  43 us
    all_gather x1, blocking collectives, local(): lax.all_gather(biases, ('img', 'seq'), axis=0, tiled=True)  37.9 us
    all_gather x1, waiting for transfers between devices, local(): lax.all_gather(w_out, ('img', 'seq'), axis=0, tiled=True)  37.2 us
    unnamed x32, waiting for transfers between devices  36.9 us
  transfers between devices with their start and end apart: 31, of which 5 were waited for; matrix products, arithmetic and copies ran while one was open for 42% of the time, Pallas kernels for 0%

commit v1 on v0

--- a/solution.py
+++ b/solution.py
@@ -3,6 +3,8 @@
 import jax
 import jax.numpy as jnp
 from jax import lax
+from jax.experimental import pallas as pl
+from jax.experimental.pallas import tpu as pltpu
 from jax.sharding import PartitionSpec as P
 
 HEADS = 16
@@ -39,6 +41,771 @@
 def join_heads(tensor):
     head_count, images_here, count, head_dim = tensor.shape
     return tensor.transpose(1, 2, 0, 3).reshape(images_here, count, head_count * head_dim)
+
+
+VMEM_BYTES = 62 * 2**20
+MESH_IDS = pl.DeviceIdType.MESH
+F32 = jnp.float32
+BF16 = jnp.bfloat16
+LANES = 128
+PIECE = 48
+BLOCK = 192
+HEAD_ROWS = 80
+NN = (((1,), (0,)), ((), ()))
+NT = (((1,), (1,)), ((), ()))
+TN = (((0,), (0,)), ((), ()))
+
+
+def mm(left, right, dims):
+    return lax.dot_general(left, right, dims, preferred_element_type=F32)
+
+
+def normalize(values):
+    average = jnp.mean(values, -1, keepdims=True)
+    centered = values - average
+    variance = jnp.mean(centered * centered, -1, keepdims=True)
+    inverse = lax.rsqrt(variance + norm_epsilon)
+    return centered * inverse, inverse
+
+
+def norm_back(grad, gain, hat, inverse):
+    scaled = grad * gain
+    first = jnp.mean(scaled, -1, keepdims=True)
+    second = jnp.mean(scaled * hat, -1, keepdims=True)
+    return inverse * (scaled - first - hat * second)
+
+
+def lane_ids(rows):
+    return lax.broadcasted_iota(jnp.int32, (rows, LANES), 1)
+
+
+def lane_window(tiles, start, width, lanes):
+    tile, offset = divmod(start, LANES)
+    if offset == 0:
+        return tiles[tile]
+    first = pltpu.roll(tiles[tile], LANES - offset, 1)
+    if offset + width <= LANES:
+        return first
+    second = pltpu.roll(tiles[tile + 1], LANES - offset, 1)
+    return jnp.where(lanes < LANES - offset, first, second)
+
+
+def layer_kernel(
+    dims,
+    off_ref, pq, po, p1, p2, tok, cot, fb_ref,
+    o_mixed, o_gtok, o_fq, o_fo, o_f1, o_f2, o_sm, o_sh,
+    wq, wo, w1, w2, rq, ro, r1, r2, tmp,
+    xs, gc, h1, h2, act, gp, dg, qkv, attm, att_t, gatt, gpj, lse,
+    g1, g2, go, gq, y1, y2, yo, yq, z1, z2, zo, zq, f1, f2, fo, fq,
+    sb_a, cr_a, xr_a, sb_b, cr_b, xr_b, pf, prm, bh, sms, smr, shs, shr,
+    ssem, rsem, lsem,
+):
+    slice_len, d, hd, f, qw, n_z = dims
+    scale = hd ** (-0.5)
+    mask_low = masked_score / scale
+    chunk = 256
+    rows = 4 * BLOCK
+    i, s = lax.axis_index("img"), lax.axis_index("seq")
+    z, y = lax.div(i, 2), lax.rem(i, 2)
+    x, c = lax.div(s, 2), lax.rem(s, 2)
+    k = 2 * c + x
+    cy = c == y
+    core_peer = (i, x * 2 + 1 - c)
+    x_peer = (i, (1 - x) * 2 + c)
+    y_peer = (z * 2 + 1 - y, s)
+    rb = wq.shape[0] // (2 * n_z)
+    own = rb // 4
+
+    def z_at(t):
+        return lax.rem(z + t + n_z, n_z)
+
+    def z_dev(t):
+        return (z_at(t) * 2 + y, s)
+
+    def s_at(t):
+        return lax.rem(s + t + 4, 4)
+
+    count = [0]
+
+    def take(n=1):
+        first = count[0]
+        count[0] += n
+        return first
+
+    def copy(src, dst, index, device):
+        return pltpu.make_async_remote_copy(
+            src, dst, ssem.at[index], rsem.at[index], device_id=device, device_id_type=MESH_IDS
+        )
+
+    sends = []
+
+    def send(src, dst, index, device):
+        made = copy(src, dst, index, device)
+        made.start()
+        sends.append(made)
+
+    def token_rows(j):
+        return pl.ds(pl.multiple_of(j * BLOCK, BLOCK), BLOCK)
+
+    def img_rows(b):
+        return pl.ds(pl.multiple_of(b * rb, 16), rb)
+
+    barrier = pltpu.get_barrier_semaphore()
+    partners = [(i, s_at(t)) for t in (1, 2, 3)] + [z_dev(t) for t in range(1, n_z)] + [y_peer]
+    for partner in partners:
+        pl.semaphore_signal(barrier, inc=1, device_id=partner, device_id_type=MESH_IDS)
+    pl.semaphore_wait(barrier, len(partners))
+
+    class Gather:
+        def __init__(self, piece, recv, full, local_index):
+            self.piece, self.recv, self.full = piece, recv, full
+            self.width = full.shape[1]
+            self.sp, self.sz, self.sy = take(4), take(n_z), take(n_z)
+            self.local = local_index
+
+        def pieces(self):
+            pltpu.make_async_copy(self.piece.at[s], self.recv.at[s], lsem.at[self.local]).start()
+            for t in (1, 2, 3):
+                to = s_at(t)
+                send(self.piece.at[to], self.recv.at[s], self.sp + t, (i, to))
+
+        def assemble(self):
+            pltpu.make_async_copy(self.piece.at[s], self.recv.at[s], lsem.at[self.local]).wait()
+            for t in (1, 2, 3):
+                came = self.recv.at[s_at(-t)]
+                copy(came, came, self.sp + t, (i, s_at(-t))).wait_recv()
+            part = rb // 4
+            for j in range(4):
+                tmp[part * j : part * j + PIECE, 0 : self.width] = self.recv[j].astype(F32)
+            self.full[img_rows(i), :] = tmp[0:rb, 0 : self.width].astype(BF16)
+
+        def block(self, t, side):
+            return self.full.at[img_rows(z_at(-t) * 2 + side)]
+
+        def along_z(self):
+            own = self.block(0, y)
+            for t in range(1, n_z):
+                send(own, own, self.sz + t, z_dev(t))
+            send(own, own, self.sy, y_peer)
+
+        def forward(self):
+            for t in range(1, n_z):
+                came = self.block(t, y)
+                copy(came, came, self.sz + t, z_dev(-t)).wait_recv()
+                send(came, came, self.sy + t, y_peer)
+
+        def finish(self):
+            for t in range(n_z):
+                came = self.block(t, 1 - y)
+                copy(came, came, self.sy + t, y_peer).wait_recv()
+
+    gather_q = Gather(pq, rq, wq, 0)
+    gather_1 = Gather(p1, r1, w1, 1)
+    gather_2 = Gather(p2, r2, w2, 2)
+    o_piece, o_z, o_y = take(), take(n_z), take(n_z)
+
+    def head_block(array, t):
+        return array.at[pl.ds(pl.multiple_of(z_at(-t) * LANES, LANES), HEAD_ROWS)]
+
+    def o_start():
+        @pl.when(cy)
+        def _():
+            pltpu.make_async_copy(po, ro.at[c], lsem.at[3]).start()
+
+        @pl.when(jnp.logical_not(cy))
+        def _():
+            copy(po, ro.at[c], o_piece, core_peer).start()
+
+    def o_assemble():
+        for h in range(4):
+            wo[h * LANES + HEAD_ROWS : (h + 1) * LANES, :] = jnp.zeros((LANES - HEAD_ROWS, d), BF16)
+
+        @pl.when(cy)
+        def _():
+            pltpu.make_async_copy(po, ro.at[c], lsem.at[3]).wait()
+            copy(po, ro.at[1 - c], o_piece, core_peer).wait_recv()
+            for j in range(2):
+                tmp[own * j : own * j + PIECE, :] = ro[j].astype(F32)
+            wo[pl.ds(pl.multiple_of(z * LANES, LANES), HEAD_ROWS), :] = tmp[0:HEAD_ROWS, :].astype(BF16)
+
+    def o_along_z():
+        @pl.when(cy)
+        def _():
+            mine = head_block(wo, 0)
+            for t in range(1, n_z):
+                copy(mine, mine, o_z + t, z_dev(t)).start()
+            copy(mine, mine, o_y, y_peer).start()
+
+    def o_forward():
+        @pl.when(cy)
+        def _():
+            for t in range(1, n_z):
+                came = head_block(wo, t)
+                copy(came, came, o_z + t, z_dev(-t)).wait_recv()
+                copy(came, came, o_y + t, y_peer).start()
+
+    def o_finish():
+        @pl.when(jnp.logical_not(cy))
+        def _():
+            for t in range(n_z):
+                came = head_block(wo, t)
+                copy(came, came, o_y + t, y_peer).wait_recv()
+
+    def o_sent():
+        @pl.when(jnp.logical_not(cy))
+        def _():
+            copy(po, ro.at[c], o_piece, core_peer).wait_send()
+
+        @pl.when(cy)
+        def _():
+            mine = head_block(wo, 0)
+            for t in range(1, n_z):
+                copy(mine, mine, o_z + t, z_dev(t)).wait_send()
+            for t in range(n_z):
+                came = head_block(wo, t)
+                copy(came, came, o_y + t, y_peer).wait_send()
+
+    class TokenGather:
+        def __init__(self, full):
+            self.full = full
+            self.sx, self.sc, self.sd = take(), take(), take()
+
+        def at(self, j):
+            return self.full.at[token_rows(j)]
+
+        def start(self, own):
+            self.own = own
+            copy(own, self.at(s), self.sx, x_peer).start()
+            copy(own, self.at(s), self.sc, core_peer).start()
+
+        def forward(self):
+            across = self.at((1 - x) * 2 + c)
+            copy(across, across, self.sx, x_peer).wait_recv()
+            copy(across, across, self.sd, core_peer).start()
+
+        def finish(self):
+            for index, j in ((self.sc, x * 2 + 1 - c), (self.sd, (1 - x) * 2 + 1 - c)):
+                copy(self.at(j), self.at(j), index, core_peer).wait_recv()
+            copy(self.own, self.at(s), self.sx, x_peer).wait_send()
+            copy(self.own, self.at(s), self.sc, core_peer).wait_send()
+            across = self.at((1 - x) * 2 + c)
+            copy(across, across, self.sd, core_peer).wait_send()
+
+    def seq_sum_start(partial, sb, cr):
+        first = take(2)
+        last = take()
+
+        def step(t, carry):
+            away = t < 2
+            j = jnp.where(away, 2 * t + 1 - c, jnp.where(t == 2, 2 * (1 - x) + c, s))
+            part = partial(j)
+
+            @pl.when(away)
+            def _():
+                sb[t] = part.astype(BF16)
+                copy(sb.at[t], cr.at[t], first + t, core_peer).start()
+
+            @pl.when(t >= 2)
+            def _():
+                pf[t - 2] = part
+
+            return carry
+
+        lax.fori_loop(0, 4, step, 0)
+        return first, last
+
+    def seq_sum_across(handle, sb, cr, xr):
+        first, last = handle
+        there = 1 - x
+        copy(cr.at[there], cr.at[there], first + there, core_peer).wait_recv()
+        sb[2] = (pf[0] + cr[there].astype(F32)).astype(BF16)
+        copy(sb.at[2], xr, last, x_peer).start()
+
+    def seq_sum_finish(handle, sb, cr, xr):
+        first, last = handle
+        copy(cr.at[x], cr.at[x], first + x, core_peer).wait_recv()
+        copy(xr, xr, last, x_peer).wait_recv()
+        for t in range(2):
+            copy(sb.at[t], cr.at[t], first + t, core_peer).wait_send()
+        copy(sb.at[2], xr, last, x_peer).wait_send()
+        return pf[1] + cr[x].astype(F32) + xr[...].astype(F32)
+
+    class Reduce:
+        def __init__(self, grad, yr, zr, fs, out):
+            self.grad, self.yr, self.zr, self.fs, self.out = grad, yr, zr, fs, out
+            self.width = grad.shape[1]
+            self.sy, self.sz, self.sp = take(n_z), take(n_z), take(4)
+
+        def at(self, t, side):
+            return img_rows(z_at(t) * 2 + side)
+
+        def across_y(self):
+            for t in (*range(1, n_z), 0):
+                send(self.grad.at[self.at(t, 1 - y)], self.yr.at[t], self.sy + t, y_peer)
+
+        def along_z(self):
+            for t in range(1, n_z):
+                copy(self.yr.at[t], self.yr.at[t], self.sy + t, y_peer).wait_recv()
+                mine = self.at(t, y)
+                self.grad[mine, :] = (self.grad[mine, :].astype(F32) + self.yr[t].astype(F32)).astype(BF16)
+                send(self.grad.at[mine], self.zr.at[t - 1], self.sz + t, z_dev(t))
+
+        def pieces(self):
+            copy(self.yr.at[0], self.yr.at[0], self.sy, y_peer).wait_recv()
+            total = self.grad[self.at(0, y), :].astype(F32) + self.yr[0].astype(F32)
+            for t in range(1, n_z):
+                came = self.zr.at[t - 1]
+                copy(came, came, self.sz + t, z_dev(-t)).wait_recv()
+                total += self.zr[t - 1].astype(F32)
+            tmp[0:rb, 0 : self.width] = total
+            part = rb // 4
+            for j in range(4):
+                self.fs[j] = tmp[part * j : part * j + PIECE, 0 : self.width].astype(BF16)
+            pltpu.make_async_copy(self.fs.at[s], self.out.at[s], lsem.at[4]).start()
+            for t in (1, 2, 3):
+                to = s_at(t)
+                send(self.fs.at[to], self.out.at[s], self.sp + t, (i, to))
+            pltpu.make_async_copy(self.fs.at[s], self.out.at[s], lsem.at[4]).wait()
+
+        def finish(self):
+            for t in (1, 2, 3):
+                came = self.out.at[s_at(-t)]
+                copy(came, came, self.sp + t, (i, s_at(-t))).wait_recv()
+
+    reduce_2 = Reduce(g2, y2, z2, f2, o_f2)
+    reduce_1 = Reduce(g1, y1, z1, f1, o_f1)
+    reduce_q = Reduce(gq, yq, zq, fq, o_fq)
+    ro_y, ro_z, ro_p = take(n_z), take(n_z), take()
+
+    def ro_across_y():
+        @pl.when(jnp.logical_not(cy))
+        def _():
+            for t in (*range(1, n_z), 0):
+                copy(head_block(go, -t), yo.at[t], ro_y + t, y_peer).start()
+
+    def ro_along_z():
+        @pl.when(cy)
+        def _():
+            for t in range(1, n_z):
+                copy(yo.at[t], yo.at[t], ro_y + t, y_peer).wait_recv()
+                mine = pl.ds(pl.multiple_of(z_at(t) * LANES, LANES), HEAD_ROWS)
+                go[mine, :] = (go[mine, :].astype(F32) + yo[t].astype(F32)).astype(BF16)
+                copy(go.at[mine], zo.at[t - 1], ro_z + t, z_dev(t)).start()
+
+    def ro_pieces():
+        @pl.when(cy)
+        def _():
+            copy(yo.at[0], yo.at[0], ro_y, y_peer).wait_recv()
+            mine = pl.ds(pl.multiple_of(z * LANES, LANES), HEAD_ROWS)
+            total = go[mine, :].astype(F32) + yo[0].astype(F32)
+            for t in range(1, n_z):
+                copy(zo.at[t - 1], zo.at[t - 1], ro_z + t, z_dev(-t)).wait_recv()
+                total += zo[t - 1].astype(F32)
+            tmp[0:HEAD_ROWS, :] = total
+            for j in range(2):
+                fo[j] = tmp[own * j : own * j + PIECE, :].astype(BF16)
+            pltpu.make_async_copy(fo.at[c], o_fo, lsem.at[5]).start()
+            copy(fo.at[1 - c], o_fo, ro_p, core_peer).start()
+            pltpu.make_async_copy(fo.at[c], o_fo, lsem.at[5]).wait()
+
+    def ro_finish():
+        @pl.when(cy)
+        def _():
+            for t in range(1, n_z):
+                copy(head_block(go, -t), zo.at[t - 1], ro_z + t, z_dev(t)).wait_send()
+            copy(fo.at[1 - c], o_fo, ro_p, core_peer).wait_send()
+
+        @pl.when(jnp.logical_not(cy))
+        def _():
+            for t in range(n_z):
+                copy(head_block(go, -t), yo.at[t], ro_y + t, y_peer).wait_send()
+            copy(o_fo, o_fo, ro_p, core_peer).wait_recv()
+
+    def real_rows(j, width):
+        t = lax.broadcasted_iota(jnp.int32, (BLOCK, width), 0)
+        position = j * slice_len + t
+        return (t < slice_len) & (position >= off_ref[0]) & (position < off_ref[0] + VALID)
+
+    tokens_in, cot_in = TokenGather(xs), TokenGather(gc)
+    gather_q.pieces()
+    pltpu.make_async_copy(tok, xs.at[token_rows(s)], lsem.at[6]).start()
+    pltpu.make_async_copy(cot, gc.at[token_rows(s)], lsem.at[7]).start()
+    tokens_in.start(tok)
+    o_start()
+    gather_1.pieces()
+    gather_2.pieces()
+    cot_in.start(cot)
+    sms[0] = jnp.zeros(sms.shape[1:], F32)
+    shs[0] = jnp.zeros(shs.shape[1:], F32)
+    tmp[...] = jnp.zeros(tmp.shape, F32)
+
+    gather_q.assemble()
+    gather_q.along_z()
+    tokens_in.forward()
+    o_assemble()
+    gather_1.assemble()
+    gather_2.assemble()
+    gather_q.forward()
+    o_along_z()
+    gather_1.along_z()
+    cot_in.forward()
+    pltpu.make_async_copy(tok, xs.at[token_rows(s)], lsem.at[6]).wait()
+    pltpu.make_async_copy(cot, gc.at[token_rows(s)], lsem.at[7]).wait()
+    tokens_in.finish()
+    cot_in.finish()
+
+    def mask_cotangent(j, carry):
+        kept = gc[token_rows(j), :].astype(F32)
+        gc[token_rows(j), :] = jnp.where(real_rows(j, d), kept, 0.0).astype(BF16)
+        return carry
+
+    lax.fori_loop(0, 4, mask_cotangent, 0)
+    gather_q.finish()
+
+    packed = 3 * 4 * hd
+    base = packed // LANES * LANES
+    columns = wq[:, base : base + LANES].astype(F32)
+    prm[...] = columns.T[packed - base : packed - base + 8, :]
+    one_lane = lane_ids(1)
+    for which, row in ((0, 3), (1, 4)):
+        tiles = [prm[row : row + 1, LANES * t : LANES * (t + 1)] for t in range(d // LANES)]
+        for head in range(d // hd):
+            bh[which, head : head + 1, :] = lane_window(tiles, head * hd, hd, one_lane)
+    gain_one, gain_two, shift_one = prm[0:1, :], prm[1:2, :], prm[2:3, :]
+    bias_out, shift_two, bias_two = prm[5:6, :], prm[6:7, :], prm[7:8, :]
+
+    lanes = lane_ids(BLOCK)
+
+    def project(j, carry):
+        hat, _ = normalize(xs[token_rows(j), :].astype(F32))
+        low = (hat * gain_one + shift_one).astype(BF16)
+        h1[token_rows(j), :] = low
+        wide = mm(low, wq[...], NN)
+        tiles = [wide[:, LANES * t : LANES * (t + 1)] for t in range(qw // LANES)]
+        key_low = jnp.where(real_rows(j, LANES), 0.0, mask_low)
+        for n in range(12):
+            kind, head = divmod(n, 4)
+            part = lane_window(tiles, n * hd, hd, lanes)
+            if kind != 1:
+                part = part + bh[kind // 2, pl.ds(4 * head + k, 1), :]
+            beside = key_low if kind == 1 else jnp.ones_like(part)
+            part = jnp.where(lanes < hd, part, jnp.where(lanes == hd, beside, 0.0))
+            qkv[n, token_rows(j), :] = part.astype(BF16)
+        return carry
+
+    lax.fori_loop(0, 4, project, 0)
+
+    sublanes = lax.broadcasted_iota(jnp.int32, (LANES, chunk), 0)
+
+    def attend(step, carry):
+        head, part = lax.div(step, rows // chunk), lax.rem(step, rows // chunk)
+        at = pl.ds(pl.multiple_of(part * chunk, chunk), chunk)
+        scores = mm(qkv[4 + head], qkv[head, at, :], NT)
+        top = jnp.max(scores, 0, keepdims=True)
+        weights = jnp.exp((scores - top) * scale).astype(BF16)
+        summed = mm(qkv[8 + head], weights, TN)
+        total = summed[hd : hd + 1, :]
+        result = jnp.where(sublanes < hd, summed / total, 0.0)
+        att_t[head, :, at] = result.astype(BF16)
+        attm[at, pl.ds(pl.multiple_of(head * LANES, LANES), LANES)] = result.T.astype(BF16)
+        lse[head, :, at] = top * scale + jnp.log(total)
+        return carry
+
+    lax.fori_loop(0, 4 * (rows // chunk), attend, 0)
+
+    o_forward()
+    o_finish()
+    sum_one = seq_sum_start(lambda j: mm(attm[token_rows(j), :], wo[...], NN), sb_a, cr_a)
+    seq_sum_across(sum_one, sb_a, cr_a, xr_a)
+    branch = seq_sum_finish(sum_one, sb_a, cr_a, xr_a)
+    o_mixed[...] = xs[token_rows(s), :].astype(F32) + branch + bias_out
+    hat, _ = normalize(o_mixed[...])
+    h2[token_rows(s), :] = (hat * gain_two + shift_two).astype(BF16)
+    h2_in = TokenGather(h2)
+    h2_in.start(h2.at[token_rows(s)])
+    h2_in.forward()
+    gather_1.forward()
+    gather_2.along_z()
+    h2_in.finish()
+    gather_1.finish()
+
+    slope = (2.0 / 3.141592653589793) ** 0.5
+
+    def widen(j, carry):
+        pre = mm(h2[token_rows(j), :], w1[...], NN) + fb_ref[...]
+        square = pre * pre
+        curve = jnp.tanh(slope * pre * (1.0 + 0.044715 * square))
+        half = 0.5 + 0.5 * curve
+        act[token_rows(j), :] = (pre * half).astype(BF16)
+        dg[token_rows(j), :] = half + 0.5 * slope * pre * (1.0 - curve * curve) * (1.0 + 0.134145 * square)
+        return carry
+
+    lax.fori_loop(0, 4, widen, 0)
+
+    def column_products(left, right, out):
+        def step(t, carry):
+            at = pl.ds(pl.multiple_of(t * LANES, LANES), LANES)
+            out[at, :] = mm(left[:, at], right[...], TN).astype(BF16)
+            return carry
+
+        lax.fori_loop(0, left.shape[1] // LANES, step, 0)
+
+    column_products(gc, act, g2)
+    gather_2.forward()
+    reduce_2.across_y()
+    gather_2.finish()
+
+    def hidden_back(j):
+        at = token_rows(j)
+        low = (mm(gc[at, :], w2[...], NN) * dg[at, :]).astype(BF16)
+        gp[at, :] = low
+        column = jnp.sum(low.astype(F32), 0, keepdims=True)
+        sms[0, pl.ds(8 + s, 1), :] += column
+        return mm(low, w1[...], NT)
+
+    sum_two = seq_sum_start(hidden_back, sb_a, cr_a)
+    seq_sum_across(sum_two, sb_a, cr_a, xr_a)
+    column_products(h2, gp, g1)
+    reduce_2.along_z()
+    reduce_1.across_y()
+    grad_h = seq_sum_finish(sum_two, sb_a, cr_a, xr_a)
+    hat, inverse = normalize(o_mixed[...])
+    kept = gc[token_rows(s), :].astype(F32)
+    grad_x = kept + norm_back(grad_h, gain_two, hat, inverse)
+    o_gtok[...] = grad_x
+    low = grad_x.astype(BF16)
+    sms[0, 1:2, :] = jnp.sum(grad_h * hat, 0, keepdims=True)
+    sms[0, 4:5, :] = jnp.sum(grad_h, 0, keepdims=True)
+    sms[0, 5:6, :] = jnp.sum(kept, 0, keepdims=True)
+    sms[0, 3:4, :] = jnp.sum(low.astype(F32), 0, keepdims=True)
+    gc[token_rows(s), :] = low
+    gb_in = TokenGather(gc)
+    gb_in.start(gc.at[token_rows(s)])
+    gb_in.forward()
+
+    sum_three = seq_sum_start(lambda j: mm(act[token_rows(j), :], w2[...], NT), sb_b, cr_b)
+    gb_in.finish()
+    seq_sum_across(sum_three, sb_b, cr_b, xr_b)
+
+    def attended_back(j, carry):
+        wide = mm(gc[token_rows(j), :], wo[...], NT).astype(BF16)
+        for head in range(4):
+            gatt[head, token_rows(j), :] = wide[:, head * LANES : (head + 1) * LANES]
+        return carry
+
+    lax.fori_loop(0, 4, attended_back, 0)
+    branch = seq_sum_finish(sum_three, sb_b, cr_b, xr_b)
+    o_mixed[...] = jnp.where(real_rows(s, d), o_mixed[...] + branch + bias_two, 0.0)
+
+    def out_products(head, carry):
+        at = pl.ds(pl.multiple_of(head * LANES, LANES), LANES)
+        go[at, :] = mm(att_t[head], gc[...], NN).astype(BF16)
+        return carry
+
+    lax.fori_loop(0, 4, out_products, 0)
+    ro_across_y()
+    reduce_1.along_z()
+    reduce_2.pieces()
+
+    wide_lanes = lane_ids(rows)
+    chunk_lanes = lane_ids(chunk)
+
+    def attend_back(head, carry):
+        grad_k = jnp.zeros((rows, LANES), F32)
+        grad_v = jnp.zeros((rows, LANES), F32)
+        grad_q = []
+        for part in range(rows // chunk):
+            at = slice(part * chunk, (part + 1) * chunk)
+            query, grad_out = qkv[head, at, :], gatt[head, at, :]
+            scores = mm(qkv[4 + head], query, NT)
+            probs = jnp.exp(scores * scale - lse[head, :, at])
+            grad_p = mm(qkv[8 + head], grad_out, NT)
+            delta = jnp.sum(probs * grad_p, 0, keepdims=True)
+            grad_s = (probs * (grad_p - delta)).astype(BF16)
+            grad_k += mm(grad_s, query, NN)
+            grad_v += mm(probs.astype(BF16), grad_out, NN)
+            grad_q.append(mm(qkv[4 + head], grad_s, TN))
+        for part in range(rows // chunk):
+            at = slice(part * chunk, (part + 1) * chunk)
+            low = jnp.where(chunk_lanes < hd, grad_q[part].T * scale, 0.0).astype(BF16)
+            qkv[head, at, :] = low
+            shs[0, pl.ds(4 * head + k, 1), :] += jnp.sum(low.astype(F32), 0, keepdims=True)
+        qkv[4 + head] = jnp.where(wide_lanes < hd, grad_k * scale, 0.0).astype(BF16)
+        low = grad_v.astype(BF16)
+        qkv[8 + head] = low
+        shs[0, pl.ds(16 + 4 * head + k, 1), :] = jnp.sum(low.astype(F32), 0, keepdims=True)
+        return carry
+
+    lax.fori_loop(0, 4, attend_back, 0)
+
+    def pack(j, carry):
+        tiles = [None] * (qw // LANES)
+        for n in range(12):
+            tile, offset = divmod(n * hd, LANES)
+            part = qkv[n, token_rows(j), :].astype(F32)
+            if offset:
+                part = pltpu.roll(part, offset, 1)
+            ends = [(tile, lanes >= offset)]
+            if offset + hd > LANES:
+                ends.append((tile + 1, lanes < offset + hd - LANES))
+            for to, where in ends:
+                kept = jnp.where(where, part, 0.0)
+                tiles[to] = kept if tiles[to] is None else tiles[to] + kept
+        for to, tile in enumerate(tiles):
+            gpj[token_rows(j), LANES * to : LANES * (to + 1)] = tile.astype(BF16)
+        return carry
+
+    lax.fori_loop(0, 4, pack, 0)
+    column_products(h1, gpj, gq)
+    reduce_q.across_y()
+    ro_along_z()
+
+    def tokens_back(j):
+        part = mm(gpj[token_rows(j), :], wq[...], NT)
+        hat, _ = normalize(xs[token_rows(j), :].astype(F32))
+        sms[0, 0:1, :] += jnp.sum(part * hat, 0, keepdims=True)
+        sms[0, 2:3, :] += jnp.sum(part, 0, keepdims=True)
+        return part
+
+    sum_four = seq_sum_start(tokens_back, sb_a, cr_a)
+    sm_at, sh_at = take(7), take(7)
+
+    def vectors(stage, slots, devices):
+        for slot, device in zip(slots, devices, strict=True):
+            send(sms.at[stage], smr.at[slot], sm_at + slot, device)
+            send(shs.at[stage], shr.at[slot], sh_at + slot, device)
+
+    def vectors_sum(stage, slots, devices):
+        for slot, device in zip(slots, devices, strict=True):
+            copy(smr.at[slot], smr.at[slot], sm_at + slot, device).wait_recv()
+            copy(shr.at[slot], shr.at[slot], sh_at + slot, device).wait_recv()
+        total, heads = sms[stage], shs[stage]
+        for slot in slots:
+            total += smr[slot]
+            heads += shr[slot]
+        return total, heads
+
+    vectors(0, (0,), (y_peer,))
+    seq_sum_across(sum_four, sb_a, cr_a, xr_a)
+    reduce_1.pieces()
+    sms[1], shs[1] = vectors_sum(0, (0,), (y_peer,))
+    vectors(1, (1, 2, 3), [z_dev(t) for t in (1, 2, 3)])
+    reduce_q.along_z()
+    sms[2], shs[2] = vectors_sum(1, (1, 2, 3), [z_dev(-t) for t in (1, 2, 3)])
+    vectors(2, (4, 5, 6), [(i, s_at(t)) for t in (1, 2, 3)])
+    grad_h = seq_sum_finish(sum_four, sb_a, cr_a, xr_a)
+    hat, inverse = normalize(xs[token_rows(s), :].astype(F32))
+    o_gtok[...] += norm_back(grad_h, gain_one, hat, inverse)
+    ro_pieces()
+    o_sm[...], o_sh[...] = vectors_sum(2, (4, 5, 6), [(i, s_at(-t)) for t in (1, 2, 3)])
+    reduce_q.pieces()
+    reduce_2.finish()
+    reduce_1.finish()
+    ro_finish()
+    o_sent()
+    reduce_q.finish()
+    for made in sends:
+        made.wait_send()
+
+
+def whole_layer(tokens, offsets, w_qkv, w_out, w_fc1, w_fc2, gains, biases, fc1_bias, cotangent):
+    _, slice_len, d = tokens.shape
+    hd = d // HEADS
+    own, wide = w_fc1.shape
+    f = wide // 4
+    f_pad = -(-f // LANES) * LANES
+    packed = 12 * hd
+    qw = -(-(packed + 8) // LANES) * LANES
+    n_z = lax.axis_size("img") // 2
+    rb = own * 4
+    rows = 4 * BLOCK
+    seq = lax.axis_index("seq")
+
+    def grow(array, *shape):
+        return jnp.pad(array, [(0, to - at) for at, to in zip(array.shape, shape, strict=True)])
+
+    heads = w_qkv.reshape(own, 3, n_z, 2, 2, hd).transpose(4, 3, 0, 1, 2, 5).reshape(4, own, packed)
+    vectors = jnp.broadcast_to(jnp.concatenate([gains, biases], 1)[None], (4, own, 8))
+    pq = grow(jnp.concatenate([heads, vectors], 2), 4, PIECE, qw)
+    p1, p2 = (grow(w.reshape(own, 4, f).transpose(1, 0, 2), 4, PIECE, f_pad) for w in (w_fc1, w_fc2))
+    po = grow(w_out, PIECE, d)
+    tok, cot = grow(tokens[0], BLOCK, d), grow(cotangent[0], BLOCK, d)
+    fb = grow(lax.dynamic_slice(fc1_bias.astype(F32), (seq * f,), (f,))[None], 1, f_pad)
+
+    hbm = pl.BlockSpec(memory_space=pl.ANY)
+    vmem = pl.BlockSpec(memory_space=pltpu.VMEM)
+    outs = [
+        ((BLOCK, d), F32, vmem),
+        ((BLOCK, d), F32, vmem),
+        ((4, PIECE, qw), BF16, hbm),
+        ((PIECE, d), BF16, hbm),
+        ((4, PIECE, f_pad), BF16, hbm),
+        ((4, PIECE, f_pad), BF16, hbm),
+        ((16, d), F32, vmem),
+        ((32, LANES), F32, vmem),
+    ]
+    low = [
+        (d, qw), (4 * LANES, d), (d, f_pad), (d, f_pad),
+        (4, PIECE, qw), (2, PIECE, d), (4, PIECE, f_pad), (4, PIECE, f_pad),
+    ]
+    scratch = [pltpu.VMEM(shape, BF16) for shape in low]
+    scratch += [pltpu.VMEM((160, max(d, f_pad)), F32)]
+    scratch += [pltpu.VMEM((rows, w), BF16) for w in (d, d, d, d, f_pad, f_pad)]
+    scratch += [pltpu.VMEM((rows, f_pad), F32)]
+    scratch += [
+        pltpu.VMEM((12, rows, LANES), BF16),
+        pltpu.VMEM((rows, 4 * LANES), BF16),
+        pltpu.VMEM((4, LANES, rows), BF16),
+        pltpu.VMEM((4, rows, LANES), BF16),
+        pltpu.VMEM((rows, qw), BF16),
+        pltpu.VMEM((4, 1, rows), F32),
+    ]
+    scratch += [pltpu.VMEM(shape, BF16) for shape in ((d, f_pad), (d, f_pad), (4 * LANES, d), (d, qw))]
+    scratch += [pltpu.VMEM((n_z, h, w), BF16) for h, w in ((rb, f_pad), (rb, f_pad), (HEAD_ROWS, d), (rb, qw))]
+    scratch += [pltpu.VMEM((n_z - 1, h, w), BF16) for h, w in ((rb, f_pad), (rb, f_pad), (HEAD_ROWS, d), (rb, qw))]
+    scratch += [pltpu.VMEM((n, PIECE, w), BF16) for n, w in ((4, f_pad), (4, f_pad), (2, d), (4, qw))]
+    for _ in range(2):
+        scratch += [pltpu.VMEM((n, BLOCK, d), BF16) for n in (3, 2)] + [pltpu.VMEM((BLOCK, d), BF16)]
+    scratch += [
+        pltpu.VMEM((2, BLOCK, d), F32),
+        pltpu.VMEM((8, d), F32),
+        pltpu.VMEM((2, 16, LANES), F32),
+        pltpu.VMEM((3, 16, d), F32),
+        pltpu.VMEM((7, 16, d), F32),
+        pltpu.VMEM((3, 32, LANES), F32),
+        pltpu.VMEM((7, 32, LANES), F32),
+        pltpu.SemaphoreType.DMA((160,)),
+        pltpu.SemaphoreType.DMA((160,)),
+        pltpu.SemaphoreType.DMA((8,)),
+    ]
+    mixed, grad_tokens, gq, go, g1, g2, small, by_head = pl.pallas_call(
+        partial(layer_kernel, (slice_len, d, hd, f, qw, n_z)),
+        out_shape=[jax.ShapeDtypeStruct(shape, kind) for shape, kind, _ in outs],
+        in_specs=[pl.BlockSpec(memory_space=pltpu.SMEM)] + [hbm] * 6 + [vmem],
+        out_specs=[spec for _, _, spec in outs],
+        scratch_shapes=scratch,
+        compiler_params=pltpu.CompilerParams(
+            collective_id=0, has_side_effects=True, vmem_limit_bytes=VMEM_BYTES
+        ),
+    )(offsets, pq, po, p1, p2, tok, cot, fb)
+
+    mixed, grad_tokens = mixed[None, :slice_len], grad_tokens[None, :slice_len]
+    grad_qkv = (
+        gq[:, :own, :packed]
+        .reshape(2, 2, own, 3, n_z, hd)
+        .transpose(2, 3, 4, 1, 0, 5)
+        .reshape(own, 3 * d)
+        .astype(F32)
+    )
+    grad_out = go[:own].astype(F32)
+    grad_fc1, grad_fc2 = (g[:, :own, :f].transpose(1, 0, 2).reshape(own, wide).astype(F32) for g in (g1, g2))
+    start = (lax.axis_index("img") * 4 + seq) * own
+    mine = lax.dynamic_slice(small[:8], (0, start), (8, own))
+    query_value = lax.dynamic_slice(by_head[:, :hd].reshape(2, d), (0, start), (2, own))
+    grad_gains = mine[:2].T
+    grad_biases = jnp.stack([mine[2], query_value[0], query_value[1], mine[3], mine[4], mine[5]], 1)
+    grad_fc1_bias = small[8:12, :f].reshape(wide)
+    return mixed, grad_tokens, grad_qkv, grad_out, grad_fc1, grad_fc2, grad_gains, grad_biases, grad_fc1_bias
 
 
 def local(tokens, offsets, w_qkv, w_out, w_fc1, w_fc2, gains, biases, fc1_bias, cotangent):
@@ -260,4 +1027,7 @@
         P(("img", "seq"), None),
         P(),
     )
-    return jax.shard_map(local, mesh=mesh, in_specs=in_specs, out_specs=out_specs, check_vma=False)
+    shards = mesh.shape["img"] * mesh.shape["seq"]
+    fits = mesh.shape["seq"] == 4 and shards == 2 * HEADS
+    plan = whole_layer if fits else local
+    return jax.shard_map(plan, mesh=mesh, in_specs=in_specs, out_specs=out_specs, check_vma=False)

time: 1660 us -> 301 us (0.18)
  blocking collectives: 961 us -> 0 us
  Pallas kernels: 0 us -> 271 us
  matrix products: 220 us -> 0 us
  local copies, waits for them, and re-layouts: 207 us -> 22.1 us
  waiting for transfers between devices: 106 us -> 0 us
  starting transfers between devices: 101 us -> 0 us
  other arithmetic: 34.8 us -> 3.1 us
    unnamed x3 -> x0, blocking collectives: 880 us -> none
    pallas_call x0 -> x1, Pallas kernels: none -> 271 us  [whole_layer(): pl.pallas_call(partial(layer_kernel, (slice_len, d, hd, f, qw, n_z)), out...]
    dot_general x124 -> x0, matrix products: 220 us -> none  [the longest x32 43 us: head_scores(): jnp.einsum('asl,aul->asu', head_query_rows, head_key_rows, preferred_elem...]
    unnamed x139 -> x24, local copies, waits for them, and re-layouts: 158 us -> 4.63 us
    unnamed x25 -> x0, starting transfers between devices: 101 us -> none
    all_gather x2 -> x0, blocking collectives: 81 us -> none  [the longest x1 43.1 us: local(): lax.all_gather(gains, ('img', 'seq'), axis=0, tiled=True)]
    all_gather x6 -> x0, waiting for transfers between devices: 69 us -> none  [the longest x1 37.2 us: local(): lax.all_gather(w_out, ('img', 'seq'), axis=0, tiled=True)]
    unnamed x32 -> x0, waiting for transfers between devices: 36.9 us -> none
  transfers between devices with their start and end apart: 31 -> 0, of which waited for: 5 -> 0; matrix products, arithmetic and copies ran while one was open for 42% -> 0% of each run, Pallas kernels for 0% -> 0%
where the time goes in v1:
time: 301 us; the launch traced here: 298 us
  Pallas kernels  271 us (90%)
  local copies, waits for them, and re-layouts  22.1 us (7%)
  other arithmetic  3.1 us (1%)
    pallas_call x1, Pallas kernels, whole_layer(): pl.pallas_call(partial(layer_kernel, (slice_len, d, hd, f, qw, n_z)), out...  271 us

profile of v1, /device:TPU:1, one launch (start us, length us, event | category | flops | bytes accessed | tf_op | source)
XLA Modules:
  0.0 297.9 jit_solution(14458449976884857973)
XLA Ops:
  0.6 0.0 copy-start.7
  1.3 0.7 pad_maximum_fusion
  2.0 0.8 dynamic-slice_convert_fusion
  2.8 0.6 pad.32.fb_ref
  3.4 0.1 copy.35
  3.5 0.0 copy-done.7
  3.5 0.7 pad.27.po
  4.2 1.2 reshape.51
  5.5 0.0 copy-start.2
  5.5 0.8 pad.28.p1
  6.3 0.3 copy-done.2
  6.6 0.3 reshape.52
  6.9 0.0 copy-start
  6.9 0.8 pad.29.p2
  7.7 0.4 copy-done
  8.1 0.8 pad.30.tok
  8.9 0.2 copy-done.5
  9.1 0.8 reshape.49
  9.9 0.2 copy.48
  10.1 0.4 reshape.50
  10.5 0.0 copy-start.1
  10.5 0.8 fusion.5.pq
  11.4 0.2 copy-done.1
  11.6 0.8 pad.31.cot
  12.4 271.2 %shard_map.169 = (f32[192,1152]{1,0:T(8,128)}, f32[192,1152]{1,0:T(8,128)}, bf16[4,48,896]{2,1,0:T(8,128)(2,1)}, bf16[48,1152]{1,0:T(8,128)(2,1)}, bf16[4,48,115...) custom-call(s32[1]{0:T(128)S(6)} %copy.51.off_ref, ...), custom_call_target="tpu_custom_call" | custom-call | tf_op jit(solution)/shard_map/pallas_call | solution.py:781
  283.5 1.5 slice_bitcast_fusion
  285.1 0.0 copy-start.10
  285.1 0.0 copy-start.9
  285.1 1.8 copy.44
  286.8 0.0 copy-done.10
  286.9 0.1 reshape.53
  286.9 0.1 constant_dynamic-slice_fusion
  287.0 0.1 constant_dynamic-slice_fusion.1
  287.1 0.6 slice_bitcast_fusion.2
  287.7 0.6 stack.3
  288.3 0.7 reshape.54
  289.0 0.7 slice_convert_fusion.1
  289.7 0.1 copy.39
  289.9 0.7 reshape.58
  290.6 0.5 copy.40
  291.1 2.2 reshape.55
  293.2 1.8 copy.43
  295.0 0.0 copy-done.4
  295.0 0.1 convert_bitcast_fusion
  295.1 0.2 copy.42
  295.3 1.2 reshape.57
  296.5 0.2 copy.41
  296.7 1.2 reshape.56
  (18 shorter events, 0.2 us)
Async XLA Ops:
  0.6 2.9 copy-start.7
  5.5 1.1 copy-start.2
  6.9 1.2 copy-start
  8.1 1.0 copy-start.5
  10.5 1.0 copy-start.1
  285.1 1.8 copy-start.10
  285.1 2.0 copy-start.9
  285.1 3.9 %copy-start.8 = (bf16[48,1152]{1,0:T(8,128)(2,1)S(1)}, bf16[48,1152]{1,0:T(8,128)(2,1)}, u32[]{:S(2)}) copy-start(bf16[48,1152]{1,0:T(8,128)(2,1)} %get-tuple-element.20) | copy-start | bytes 331780
  286.9 2.8 copy-start.6
  293.2 1.8 copy-start.3
  293.2 1.8 copy-start.4

commit v2 on v1

--- a/solution.py
+++ b/solution.py
@@ -96,7 +96,7 @@
     o_mixed, o_gtok, o_fq, o_fo, o_f1, o_f2, o_sm, o_sh,
     wq, wo, w1, w2, rq, ro, r1, r2, tmp,
     xs, gc, h1, h2, act, gp, dg, qkv, attm, att_t, gatt, gpj, lse,
-    g1, g2, go, gq, y1, y2, yo, yq, z1, z2, zo, zq, f1, f2, fo, fq,
+    g1, g2, go, gq, y1, y2, yo, yq, z1, z2, zo, zq,
     sb_a, cr_a, xr_a, sb_b, cr_b, xr_b, pf, prm, bh, sms, smr, shs, shr,
     ssem, rsem, lsem,
 ):
@@ -122,6 +122,18 @@
     def z_dev(t):
         return (z_at(t) * 2 + y, s)
 
+    def z_to(zt):
+        return (zt * 2 + y, s)
+
+    near = (
+        z,
+        jnp.where(z == 0, 1, z - 1),
+        jnp.where(z == 0, 2, jnp.where(z == 3, 1, z + 1)),
+        jnp.where(z <= 1, 3, 0),
+    )
+    middle = (z == 1) | (z == 2)
+    end = jnp.where(z == 1, 0, 3)
+
     def s_at(t):
         return lax.rem(s + t + 4, 4)
 
@@ -132,15 +144,15 @@
         count[0] += n
         return first
 
-    def copy(src, dst, index, device):
+    def copy(src, dst, index, device, at=None):
         return pltpu.make_async_remote_copy(
-            src, dst, ssem.at[index], rsem.at[index], device_id=device, device_id_type=MESH_IDS
+            src, dst, ssem.at[index], rsem.at[index if at is None else at], device_id=device, device_id_type=MESH_IDS
         )
 
     sends = []
 
-    def send(src, dst, index, device):
-        made = copy(src, dst, index, device)
+    def send(src, dst, index, device, at=None):
+        made = copy(src, dst, index, device, at)
         made.start()
         sends.append(made)
 
@@ -179,25 +191,45 @@
                 tmp[part * j : part * j + PIECE, 0 : self.width] = self.recv[j].astype(F32)
             self.full[img_rows(i), :] = tmp[0:rb, 0 : self.width].astype(BF16)
 
-        def block(self, t, side):
-            return self.full.at[img_rows(z_at(-t) * 2 + side)]
+        def block(self, zb, side):
+            return self.full.at[img_rows(zb * 2 + side)]
 
         def along_z(self):
-            own = self.block(0, y)
-            for t in range(1, n_z):
-                send(own, own, self.sz + t, z_dev(t))
-            send(own, own, self.sy, y_peer)
-
-        def forward(self):
-            for t in range(1, n_z):
-                came = self.block(t, y)
-                copy(came, came, self.sz + t, z_dev(-t)).wait_recv()
-                send(came, came, self.sy + t, y_peer)
+            own = self.block(z, y)
+            for u in (1, 2):
+                send(own, own, self.sz + u, z_to(near[u]), self.sz + z)
+
+            @pl.when(middle)
+            def _():
+                copy(own, own, self.sz + 3, z_to(near[3]), self.sz + z).start()
+
+        def across_y(self):
+            own = self.block(z, y)
+            send(own, own, self.sy, y_peer, self.sy + z)
+
+        def forward(self, *steps):
+            for u in steps:
+                zb = near[u]
+                came = self.block(zb, y)
+                copy(came, came, self.sz, z_to(zb), self.sz + zb).wait_recv()
+                send(came, came, self.sy + u, y_peer, self.sy + zb)
+                if u == 3:
+
+                    @pl.when(middle)
+                    def _():
+                        copy(came, came, self.sz, z_to(end), self.sz + zb).start()
 
         def finish(self):
-            for t in range(n_z):
-                came = self.block(t, 1 - y)
-                copy(came, came, self.sy + t, y_peer).wait_recv()
+            for zb in range(n_z):
+                came = self.block(zb, 1 - y)
+                copy(came, came, self.sy, y_peer, self.sy + zb).wait_recv()
+
+        def sent(self):
+            @pl.when(middle)
+            def _():
+                own, came = self.block(z, y), self.block(near[3], y)
+                copy(own, own, self.sz + 3, z_to(near[3]), self.sz + z).wait_send()
+                copy(came, came, self.sz, z_to(end), self.sz + near[3]).wait_send()
 
     gather_q = Gather(pq, rq, wq, 0)
     gather_1 = Gather(p1, r1, w1, 1)
@@ -336,28 +368,58 @@
             self.width = grad.shape[1]
             self.sy, self.sz, self.sp = take(n_z), take(n_z), take(4)
 
-        def at(self, t, side):
-            return img_rows(z_at(t) * 2 + side)
+        def at(self, zb, side):
+            return img_rows(zb * 2 + side)
 
         def across_y(self):
-            for t in (*range(1, n_z), 0):
-                send(self.grad.at[self.at(t, 1 - y)], self.yr.at[t], self.sy + t, y_peer)
-
-        def along_z(self):
-            for t in range(1, n_z):
-                copy(self.yr.at[t], self.yr.at[t], self.sy + t, y_peer).wait_recv()
-                mine = self.at(t, y)
-                self.grad[mine, :] = (self.grad[mine, :].astype(F32) + self.yr[t].astype(F32)).astype(BF16)
-                send(self.grad.at[mine], self.zr.at[t - 1], self.sz + t, z_dev(t))
+            for u in (3, 2, 1, 0):
+                rows_there = self.grad.at[self.at(near[u], 1 - y)]
+                send(rows_there, self.yr.at[u], self.sy + u, y_peer)
+
+        def along_z(self, *steps):
+            for u in steps:
+                copy(self.yr.at[u], self.yr.at[u], self.sy + u, y_peer).wait_recv()
+                mine = self.at(near[u], y)
+                self.grad[mine, :] = (self.grad[mine, :].astype(F32) + self.yr[u].astype(F32)).astype(BF16)
+                if u < 3:
+                    send(self.grad.at[mine], self.zr.at[z], self.sz + u, z_to(near[u]), self.sz + z)
+                else:
+
+                    @pl.when(jnp.logical_not(middle))
+                    def _():
+                        self.far().start()
+
+        def far(self):
+            rows_far = self.grad.at[self.at(near[3], y)]
+            return copy(rows_far, self.zr.at[near[1]], self.sz + 3, z_to(near[1]), self.sz + near[1])
+
+        def onward(self):
+            rows_far = self.grad.at[self.at(near[3], y)]
+            return copy(rows_far, self.zr.at[z], self.sz + 3, z_to(near[3]), self.sz + z)
+
+        def relay(self):
+            @pl.when(middle)
+            def _():
+                mine = self.at(near[3], y)
+                copy(self.zr.at[z], self.zr.at[z], self.sz, z_to(end), self.sz + z).wait_recv()
+                self.grad[mine, :] = (self.grad[mine, :].astype(F32) + self.zr[z].astype(F32)).astype(BF16)
+                self.onward().start()
+
+        def came_z(self, u):
+            zb = near[u]
+            copy(self.zr.at[zb], self.zr.at[zb], self.sz, z_to(zb), self.sz + zb).wait_recv()
+            tmp[0:rb, 0 : self.width] += self.zr[zb].astype(F32)
 
         def pieces(self):
             copy(self.yr.at[0], self.yr.at[0], self.sy, y_peer).wait_recv()
-            total = self.grad[self.at(0, y), :].astype(F32) + self.yr[0].astype(F32)
-            for t in range(1, n_z):
-                came = self.zr.at[t - 1]
-                copy(came, came, self.sz + t, z_dev(-t)).wait_recv()
-                total += self.zr[t - 1].astype(F32)
-            tmp[0:rb, 0 : self.width] = total
+            tmp[0:rb, 0 : self.width] = self.grad[self.at(z, y), :].astype(F32) + self.yr[0].astype(F32)
+            self.came_z(1)
+            self.came_z(2)
+
+            @pl.when(middle)
+            def _():
+                self.came_z(3)
+
             part = rb // 4
             for j in range(4):
                 self.fs[j] = tmp[part * j : part * j + PIECE, 0 : self.width].astype(BF16)
@@ -367,14 +429,23 @@
                 send(self.fs.at[to], self.out.at[s], self.sp + t, (i, to))
             pltpu.make_async_copy(self.fs.at[s], self.out.at[s], lsem.at[4]).wait()
 
+        def sent(self):
+            @pl.when(middle)
+            def _():
+                self.onward().wait_send()
+
+            @pl.when(jnp.logical_not(middle))
+            def _():
+                self.far().wait_send()
+
         def finish(self):
             for t in (1, 2, 3):
                 came = self.out.at[s_at(-t)]
                 copy(came, came, self.sp + t, (i, s_at(-t))).wait_recv()
 
-    reduce_2 = Reduce(g2, y2, z2, f2, o_f2)
-    reduce_1 = Reduce(g1, y1, z1, f1, o_f1)
-    reduce_q = Reduce(gq, yq, zq, fq, o_fq)
+    reduce_2 = Reduce(g2, y2, z2, r2, o_f2)
+    reduce_1 = Reduce(g1, y1, z1, r1, o_f1)
+    reduce_q = Reduce(gq, yq, zq, rq, o_fq)
     ro_y, ro_z, ro_p = take(n_z), take(n_z), take()
 
     def ro_across_y():
@@ -403,17 +474,17 @@
                 total += zo[t - 1].astype(F32)
             tmp[0:HEAD_ROWS, :] = total
             for j in range(2):
-                fo[j] = tmp[own * j : own * j + PIECE, :].astype(BF16)
-            pltpu.make_async_copy(fo.at[c], o_fo, lsem.at[5]).start()
-            copy(fo.at[1 - c], o_fo, ro_p, core_peer).start()
-            pltpu.make_async_copy(fo.at[c], o_fo, lsem.at[5]).wait()
+                ro[j] = tmp[own * j : own * j + PIECE, :].astype(BF16)
+            pltpu.make_async_copy(ro.at[c], o_fo, lsem.at[5]).start()
+            copy(ro.at[1 - c], o_fo, ro_p, core_peer).start()
+            pltpu.make_async_copy(ro.at[c], o_fo, lsem.at[5]).wait()
 
     def ro_finish():
         @pl.when(cy)
         def _():
             for t in range(1, n_z):
                 copy(head_block(go, -t), zo.at[t - 1], ro_z + t, z_dev(t)).wait_send()
-            copy(fo.at[1 - c], o_fo, ro_p, core_peer).wait_send()
+            copy(ro.at[1 - c], o_fo, ro_p, core_peer).wait_send()
 
         @pl.when(jnp.logical_not(cy))
         def _():
@@ -441,25 +512,24 @@
 
     gather_q.assemble()
     gather_q.along_z()
+    gather_q.across_y()
+    o_assemble()
     tokens_in.forward()
-    o_assemble()
+    gather_q.forward(1)
     gather_1.assemble()
-    gather_2.assemble()
-    gather_q.forward()
+    gather_q.forward(2, 3)
     o_along_z()
     gather_1.along_z()
-    cot_in.forward()
+    gather_1.across_y()
+    gather_2.assemble()
+    gather_2.across_y()
     pltpu.make_async_copy(tok, xs.at[token_rows(s)], lsem.at[6]).wait()
-    pltpu.make_async_copy(cot, gc.at[token_rows(s)], lsem.at[7]).wait()
     tokens_in.finish()
-    cot_in.finish()
-
     def mask_cotangent(j, carry):
         kept = gc[token_rows(j), :].astype(F32)
         gc[token_rows(j), :] = jnp.where(real_rows(j, d), kept, 0.0).astype(BF16)
         return carry
 
-    lax.fori_loop(0, 4, mask_cotangent, 0)
     gather_q.finish()
 
     packed = 3 * 4 * hd
@@ -494,6 +564,7 @@
         return carry
 
     lax.fori_loop(0, 4, project, 0)
+    o_forward()
 
     sublanes = lax.broadcasted_iota(jnp.int32, (LANES, chunk), 0)
 
@@ -513,19 +584,27 @@
 
     lax.fori_loop(0, 4 * (rows // chunk), attend, 0)
 
-    o_forward()
+    gather_1.forward(1)
+    cot_in.forward()
+    pltpu.make_async_copy(cot, gc.at[token_rows(s)], lsem.at[7]).wait()
+    cot_in.finish()
+    lax.fori_loop(0, 4, mask_cotangent, 0)
+
+    gather_1.forward(2)
     o_finish()
     sum_one = seq_sum_start(lambda j: mm(attm[token_rows(j), :], wo[...], NN), sb_a, cr_a)
     seq_sum_across(sum_one, sb_a, cr_a, xr_a)
+    gather_1.forward(3)
+    gather_2.along_z()
     branch = seq_sum_finish(sum_one, sb_a, cr_a, xr_a)
     o_mixed[...] = xs[token_rows(s), :].astype(F32) + branch + bias_out
     hat, _ = normalize(o_mixed[...])
     h2[token_rows(s), :] = (hat * gain_two + shift_two).astype(BF16)
     h2_in = TokenGather(h2)
     h2_in.start(h2.at[token_rows(s)])
+    gather_2.forward(1)
     h2_in.forward()
-    gather_1.forward()
-    gather_2.along_z()
+    gather_2.forward(2, 3)
     h2_in.finish()
     gather_1.finish()
 
@@ -551,7 +630,6 @@
         lax.fori_loop(0, left.shape[1] // LANES, step, 0)
 
     column_products(gc, act, g2)
-    gather_2.forward()
     reduce_2.across_y()
     gather_2.finish()
 
@@ -566,8 +644,9 @@
     sum_two = seq_sum_start(hidden_back, sb_a, cr_a)
     seq_sum_across(sum_two, sb_a, cr_a, xr_a)
     column_products(h2, gp, g1)
-    reduce_2.along_z()
     reduce_1.across_y()
+    reduce_2.along_z(3)
+    reduce_2.along_z(2)
     grad_h = seq_sum_finish(sum_two, sb_a, cr_a, xr_a)
     hat, inverse = normalize(o_mixed[...])
     kept = gc[token_rows(s), :].astype(F32)
@@ -581,11 +660,12 @@
     gc[token_rows(s), :] = low
     gb_in = TokenGather(gc)
     gb_in.start(gc.at[token_rows(s)])
+
+    sum_three = seq_sum_start(lambda j: mm(act[token_rows(j), :], w2[...], NT), sb_b, cr_b)
+    seq_sum_across(sum_three, sb_b, cr_b, xr_b)
+    reduce_2.along_z(1)
     gb_in.forward()
-
-    sum_three = seq_sum_start(lambda j: mm(act[token_rows(j), :], w2[...], NT), sb_b, cr_b)
     gb_in.finish()
-    seq_sum_across(sum_three, sb_b, cr_b, xr_b)
 
     def attended_back(j, carry):
         wide = mm(gc[token_rows(j), :], wo[...], NT).astype(BF16)
@@ -594,8 +674,6 @@
         return carry
 
     lax.fori_loop(0, 4, attended_back, 0)
-    branch = seq_sum_finish(sum_three, sb_b, cr_b, xr_b)
-    o_mixed[...] = jnp.where(real_rows(s, d), o_mixed[...] + branch + bias_two, 0.0)
 
     def out_products(head, carry):
         at = pl.ds(pl.multiple_of(head * LANES, LANES), LANES)
@@ -604,8 +682,9 @@
 
     lax.fori_loop(0, 4, out_products, 0)
     ro_across_y()
-    reduce_1.along_z()
-    reduce_2.pieces()
+    reduce_2.relay()
+    branch = seq_sum_finish(sum_three, sb_b, cr_b, xr_b)
+    o_mixed[...] = jnp.where(real_rows(s, d), o_mixed[...] + branch + bias_two, 0.0)
 
     wide_lanes = lane_ids(rows)
     chunk_lanes = lane_ids(chunk)
@@ -636,7 +715,12 @@
         shs[0, pl.ds(16 + 4 * head + k, 1), :] = jnp.sum(low.astype(F32), 0, keepdims=True)
         return carry
 
-    lax.fori_loop(0, 4, attend_back, 0)
+    reduce_1.along_z(3)
+    lax.fori_loop(0, 2, attend_back, 0)
+    reduce_1.along_z(2)
+    lax.fori_loop(2, 4, attend_back, 0)
+    reduce_1.along_z(1)
+    reduce_1.relay()
 
     def pack(j, carry):
         tiles = [None] * (qw // LANES)
@@ -659,6 +743,7 @@
     column_products(h1, gpj, gq)
     reduce_q.across_y()
     ro_along_z()
+    reduce_2.pieces()
 
     def tokens_back(j):
         part = mm(gpj[token_rows(j), :], wq[...], NT)
@@ -687,15 +772,17 @@
 
     vectors(0, (0,), (y_peer,))
     seq_sum_across(sum_four, sb_a, cr_a, xr_a)
-    reduce_1.pieces()
     sms[1], shs[1] = vectors_sum(0, (0,), (y_peer,))
     vectors(1, (1, 2, 3), [z_dev(t) for t in (1, 2, 3)])
-    reduce_q.along_z()
+    reduce_1.pieces()
+    reduce_q.along_z(3)
     sms[2], shs[2] = vectors_sum(1, (1, 2, 3), [z_dev(-t) for t in (1, 2, 3)])
     vectors(2, (4, 5, 6), [(i, s_at(t)) for t in (1, 2, 3)])
     grad_h = seq_sum_finish(sum_four, sb_a, cr_a, xr_a)
     hat, inverse = normalize(xs[token_rows(s), :].astype(F32))
     o_gtok[...] += norm_back(grad_h, gain_one, hat, inverse)
+    reduce_q.along_z(2, 1)
+    reduce_q.relay()
     ro_pieces()
     o_sm[...], o_sh[...] = vectors_sum(2, (4, 5, 6), [(i, s_at(-t)) for t in (1, 2, 3)])
     reduce_q.pieces()
@@ -704,6 +791,8 @@
     ro_finish()
     o_sent()
     reduce_q.finish()
+    for part in (gather_q, gather_1, gather_2, reduce_q, reduce_1, reduce_2):
+        part.sent()
     for made in sends:
         made.wait_send()
 
@@ -762,8 +851,7 @@
     ]
     scratch += [pltpu.VMEM(shape, BF16) for shape in ((d, f_pad), (d, f_pad), (4 * LANES, d), (d, qw))]
     scratch += [pltpu.VMEM((n_z, h, w), BF16) for h, w in ((rb, f_pad), (rb, f_pad), (HEAD_ROWS, d), (rb, qw))]
-    scratch += [pltpu.VMEM((n_z - 1, h, w), BF16) for h, w in ((rb, f_pad), (rb, f_pad), (HEAD_ROWS, d), (rb, qw))]
-    scratch += [pltpu.VMEM((n, PIECE, w), BF16) for n, w in ((4, f_pad), (4, f_pad), (2, d), (4, qw))]
+    scratch += [pltpu.VMEM((n_z, h, w), BF16) for h, w in ((rb, f_pad), (rb, f_pad), (HEAD_ROWS, d), (rb, qw))]
     for _ in range(2):
         scratch += [pltpu.VMEM((n, BLOCK, d), BF16) for n in (3, 2)] + [pltpu.VMEM((BLOCK, d), BF16)]
     scratch += [

time: 301 us -> 260 us (0.86)
  Pallas kernels: 271 us -> 232 us
    pallas_call x1, Pallas kernels: 271 us -> 232 us  [whole_layer(): pl.pallas_call(partial(layer_kernel, (slice_len, d, hd, f, qw, n_z)), out...]
where the time goes in v2:
time: 260 us; the launch traced here: 259 us
  Pallas kernels  232 us (89%)
  local copies, waits for them, and re-layouts  22.1 us (8%)
  other arithmetic  3.1 us (1%)
    pallas_call x1, Pallas kernels, whole_layer(): pl.pallas_call(partial(layer_kernel, (slice_len, d, hd, f, qw, n_z)), out...  232 us

profile of v2, /device:TPU:1, one launch (start us, length us, event | category | flops | bytes accessed | tf_op | source)
XLA Modules:
  0.0 259.2 jit_solution(14011950655789419071)
XLA Ops:
  0.6 0.0 copy-start.7
  1.3 0.7 pad_maximum_fusion
  2.0 0.8 dynamic-slice_convert_fusion
  2.8 0.6 pad.32.fb_ref
  3.4 0.1 copy.35
  3.5 0.0 copy-done.7
  3.5 0.7 pad.27.po
  4.2 1.2 reshape.51
  5.5 0.0 copy-start.2
  5.5 0.8 pad.28.p1
  6.3 0.3 copy-done.2
  6.6 0.3 reshape.52
  6.9 0.0 copy-start
  6.9 0.8 pad.29.p2
  7.7 0.4 copy-done
  8.1 0.8 pad.30.tok
  8.9 0.2 copy-done.5
  9.1 0.8 reshape.49
  9.9 0.2 copy.48
  10.1 0.4 reshape.50
  10.5 0.0 copy-start.1
  10.5 0.8 fusion.5.pq
  11.4 0.2 copy-done.1
  11.6 0.8 pad.31.cot
  12.4 232.5 %shard_map.169 = (f32[192,1152]{1,0:T(8,128)}, f32[192,1152]{1,0:T(8,128)}, bf16[4,48,896]{2,1,0:T(8,128)(2,1)}, bf16[48,1152]{1,0:T(8,128)(2,1)}, bf16[4,48,115...) custom-call(s32[1]{0:T(128)S(6)} %copy.51.off_ref, ...), custom_call_target="tpu_custom_call" | custom-call | tf_op jit(solution)/shard_map/pallas_call | solution.py:869
  244.8 1.5 slice_bitcast_fusion
  246.4 0.0 copy-start.10
  246.4 0.0 copy-start.9
  246.4 0.0 copy-start.8
  246.4 1.8 copy.44
  248.2 0.1 reshape.53
  248.2 0.1 constant_dynamic-slice_fusion
  248.3 0.1 constant_dynamic-slice_fusion.1
  248.4 0.6 slice_bitcast_fusion.2
  249.0 0.6 stack.3
  249.6 0.7 reshape.54
  250.3 0.7 slice_convert_fusion.1
  251.0 0.1 copy.39
  251.2 0.7 reshape.58
  251.9 0.5 copy.40
  252.4 2.2 reshape.55
  254.5 1.8 copy.43
  256.3 0.0 copy-done.3
  256.3 0.1 convert_bitcast_fusion
  256.4 0.2 copy.42
  256.6 1.2 reshape.57
  257.8 0.2 copy.41
  258.0 1.2 reshape.56
  (18 shorter events, 0.2 us)
Async XLA Ops:
  0.6 2.9 %copy-start.7 = (bf16[36,1152]{1,0:T(8,128)(2,1)S(1)}, bf16[36,1152]{1,0:T(8,128)(2,1)}, u32[]{:S(2)}) copy-start(bf16[36,1152]{1,0:T(8,128)(2,1)} %param.13) | copy-start | bytes 248836
  5.5 1.1 copy-start.2
  6.9 1.2 copy-start
  8.1 1.0 copy-start.5
  10.5 1.0 copy-start.1
  246.4 1.8 copy-start.10
  246.4 2.0 copy-start.9
  246.4 3.9 %copy-start.8 = (bf16[48,1152]{1,0:T(8,128)(2,1)S(1)}, bf16[48,1152]{1,0:T(8,128)(2,1)}, u32[]{:S(2)}) copy-start(bf16[48,1152]{1,0:T(8,128)(2,1)} %get-tuple-element.20) | copy-start | bytes 331780
  248.2 2.8 %copy-start.6 = (bf16[4,48,896]{2,1,0:T(8,128)(2,1)S(1)}, bf16[4,48,896]{2,1,0:T(8,128)(2,1)}, u32[]{:S(2)}) copy-start(bf16[4,48,896]{2,1,0:T(8,128)(2,1)} %get-tuple-element.19) | copy-start | bytes 1032196
  254.5 1.8 copy-start.3
  254.5 1.8 copy-start.4

commit v3 on v2

--- a/solution.py
+++ b/solution.py
@@ -48,6 +48,7 @@
 F32 = jnp.float32
 BF16 = jnp.bfloat16
 LANES = 128
+SLIVER = 16
 PIECE = 48
 BLOCK = 192
 HEAD_ROWS = 80
@@ -96,7 +97,7 @@
     o_mixed, o_gtok, o_fq, o_fo, o_f1, o_f2, o_sm, o_sh,
     wq, wo, w1, w2, rq, ro, r1, r2, tmp,
     xs, gc, h1, h2, act, gp, dg, qkv, attm, att_t, gatt, gpj, lse,
-    g1, g2, go, gq, y1, y2, yo, yq, z1, z2, zo, zq,
+    g1, g2, go, gq, y1, y2, yo, yq, z1, z2, zo, zq, s1, s2,
     sb_a, cr_a, xr_a, sb_b, cr_b, xr_b, pf, prm, bh, sms, smr, shs, shr,
     ssem, rsem, lsem,
 ):
@@ -162,6 +163,12 @@
     def img_rows(b):
         return pl.ds(pl.multiple_of(b * rb, 16), rb)
 
+    def most_rows(b, most=rb - SLIVER):
+        return pl.ds(pl.multiple_of(b * rb, 16), most)
+
+    def sliver_rows(b):
+        return pl.ds(pl.multiple_of(b * rb + rb - SLIVER, 16), SLIVER)
+
     barrier = pltpu.get_barrier_semaphore()
     partners = [(i, s_at(t)) for t in (1, 2, 3)] + [z_dev(t) for t in range(1, n_z)] + [y_peer]
     for partner in partners:
@@ -172,7 +179,7 @@
         def __init__(self, piece, recv, full, local_index):
             self.piece, self.recv, self.full = piece, recv, full
             self.width = full.shape[1]
-            self.sp, self.sz, self.sy = take(4), take(n_z), take(n_z)
+            self.sp, self.sz, self.sy, self.ss = take(4), take(n_z), take(n_z), take(n_z)
             self.local = local_index
 
         def pieces(self):
@@ -194,6 +201,18 @@
         def block(self, zb, side):
             return self.full.at[img_rows(zb * 2 + side)]
 
+        def most(self, zb, side):
+            return self.full.at[most_rows(zb * 2 + side)]
+
+        def sliver(self, zb, side):
+            return self.full.at[sliver_rows(zb * 2 + side)]
+
+        def slivers(self):
+            whole, part = self.block(z, 1 - y), self.sliver(z, 1 - y)
+            copy(whole, whole, self.sy, y_peer, self.sy + z).wait_recv()
+            for u in (1, 2, 3):
+                send(part, part, self.ss + u, z_to(near[u]), self.ss + z)
+
         def along_z(self):
             own = self.block(z, y)
             for u in (1, 2):
@@ -212,17 +231,30 @@
                 zb = near[u]
                 came = self.block(zb, y)
                 copy(came, came, self.sz, z_to(zb), self.sz + zb).wait_recv()
-                send(came, came, self.sy + u, y_peer, self.sy + zb)
-                if u == 3:
-
-                    @pl.when(middle)
-                    def _():
-                        copy(came, came, self.sz, z_to(end), self.sz + zb).start()
+                came = self.most(zb, y)
+                copy(came, came, self.sy + u, y_peer, self.sy + zb).start()
+
+        def relay(self):
+            @pl.when(middle)
+            def _():
+                came = self.block(near[3], y)
+                copy(came, came, self.sz, z_to(end), self.sz + near[3]).wait_recv()
+                copy(came, came, self.sz, z_to(end), self.sz + near[3]).start()
+                came = self.most(near[3], y)
+                copy(came, came, self.sy + 3, y_peer, self.sy + near[3]).start()
+
+        def forward_far(self):
+            @pl.when(jnp.logical_not(middle))
+            def _():
+                self.forward(3)
 
         def finish(self):
-            for zb in range(n_z):
-                came = self.block(zb, 1 - y)
+            for u in (1, 2, 3):
+                zb = near[u]
+                came = self.most(zb, 1 - y)
                 copy(came, came, self.sy, y_peer, self.sy + zb).wait_recv()
+                came = self.sliver(zb, 1 - y)
+                copy(came, came, self.ss, z_to(zb), self.ss + zb).wait_recv()
 
         def sent(self):
             @pl.when(middle)
@@ -230,6 +262,10 @@
                 own, came = self.block(z, y), self.block(near[3], y)
                 copy(own, own, self.sz + 3, z_to(near[3]), self.sz + z).wait_send()
                 copy(came, came, self.sz, z_to(end), self.sz + near[3]).wait_send()
+
+            for u in (1, 2, 3):
+                came = self.most(near[u], y)
+                copy(came, came, self.sy + u, y_peer, self.sy + near[u]).wait_send()
 
     gather_q = Gather(pq, rq, wq, 0)
     gather_1 = Gather(p1, r1, w1, 1)
@@ -363,24 +399,41 @@
         return pf[1] + cr[x].astype(F32) + xr[...].astype(F32)
 
     class Reduce:
-        def __init__(self, grad, yr, zr, fs, out):
-            self.grad, self.yr, self.zr, self.fs, self.out = grad, yr, zr, fs, out
+        def __init__(self, grad, yr, zr, zs, fs, out):
+            self.grad, self.yr, self.zr, self.zs, self.fs, self.out = grad, yr, zr, zs, fs, out
+            self.most = rb if zs is None else rb - SLIVER
             self.width = grad.shape[1]
-            self.sy, self.sz, self.sp = take(n_z), take(n_z), take(4)
+            self.sy, self.sz, self.sp, self.ss = take(n_z), take(n_z), take(4), take(n_z)
 
         def at(self, zb, side):
             return img_rows(zb * 2 + side)
 
         def across_y(self):
-            for u in (3, 2, 1, 0):
-                rows_there = self.grad.at[self.at(near[u], 1 - y)]
-                send(rows_there, self.yr.at[u], self.sy + u, y_peer)
+            for u in (3, 2, 1):
+                b = near[u] * 2 + 1 - y
+                send(self.grad.at[most_rows(b, self.most)], self.yr.at[u, 0 : self.most], self.sy + u, y_peer)
+                if self.zs is not None:
+                    send(self.grad.at[sliver_rows(b)], self.zs.at[z], self.ss + u, z_to(near[u]), self.ss + z)
+            if self.zs is None:
+                send(self.grad.at[img_rows(z * 2 + 1 - y)], self.yr.at[0], self.sy, y_peer)
+
+        def across_last(self):
+            b = z * 2 + 1 - y
+            part = self.grad[sliver_rows(b), :].astype(F32)
+            for u in (1, 2, 3):
+                zb = near[u]
+                copy(self.zs.at[zb], self.zs.at[zb], self.ss, z_to(zb), self.ss + zb).wait_recv()
+                part += self.zs[zb].astype(F32)
+            self.grad[sliver_rows(b), :] = part.astype(BF16)
+            send(self.grad.at[img_rows(b)], self.yr.at[0], self.sy, y_peer)
 
         def along_z(self, *steps):
             for u in steps:
-                copy(self.yr.at[u], self.yr.at[u], self.sy + u, y_peer).wait_recv()
-                mine = self.at(near[u], y)
-                self.grad[mine, :] = (self.grad[mine, :].astype(F32) + self.yr[u].astype(F32)).astype(BF16)
+                came = self.yr.at[u, 0 : self.most]
+                copy(came, came, self.sy + u, y_peer).wait_recv()
+                mine, most = self.at(near[u], y), most_rows(near[u] * 2 + y, self.most)
+                added = self.yr[u, 0 : self.most, :].astype(F32)
+                self.grad[most, :] = (self.grad[most, :].astype(F32) + added).astype(BF16)
                 if u < 3:
                     send(self.grad.at[mine], self.zr.at[z], self.sz + u, z_to(near[u]), self.sz + z)
                 else:
@@ -443,9 +496,9 @@
                 came = self.out.at[s_at(-t)]
                 copy(came, came, self.sp + t, (i, s_at(-t))).wait_recv()
 
-    reduce_2 = Reduce(g2, y2, z2, r2, o_f2)
-    reduce_1 = Reduce(g1, y1, z1, r1, o_f1)
-    reduce_q = Reduce(gq, yq, zq, rq, o_fq)
+    reduce_2 = Reduce(g2, y2, z2, s2, r2, o_f2)
+    reduce_1 = Reduce(g1, y1, z1, s1, r1, o_f1)
+    reduce_q = Reduce(gq, yq, zq, None, rq, o_fq)
     ro_y, ro_z, ro_p = take(n_z), take(n_z), take()
 
     def ro_across_y():
@@ -514,15 +567,20 @@
     gather_q.along_z()
     gather_q.across_y()
     o_assemble()
+    o_along_z()
+    gather_q.forward(1)
     tokens_in.forward()
-    gather_q.forward(1)
     gather_1.assemble()
-    gather_q.forward(2, 3)
-    o_along_z()
+    gather_q.slivers()
+    gather_q.forward(2)
+    gather_q.relay()
     gather_1.along_z()
     gather_1.across_y()
     gather_2.assemble()
+    gather_q.forward_far()
+    o_forward()
     gather_2.across_y()
+    cot_in.forward()
     pltpu.make_async_copy(tok, xs.at[token_rows(s)], lsem.at[6]).wait()
     tokens_in.finish()
     def mask_cotangent(j, carry):
@@ -564,8 +622,8 @@
         return carry
 
     lax.fori_loop(0, 4, project, 0)
-    o_forward()
-
+    gather_1.slivers()
+    gather_2.along_z()
     sublanes = lax.broadcasted_iota(jnp.int32, (LANES, chunk), 0)
 
     def attend(step, carry):
@@ -582,10 +640,12 @@
         lse[head, :, at] = top * scale + jnp.log(total)
         return carry
 
-    lax.fori_loop(0, 4 * (rows // chunk), attend, 0)
-
+    lax.fori_loop(0, 2 * (rows // chunk), attend, 0)
     gather_1.forward(1)
-    cot_in.forward()
+    lax.fori_loop(2 * (rows // chunk), 4 * (rows // chunk), attend, 0)
+    gather_1.relay()
+    gather_2.slivers()
+
     pltpu.make_async_copy(cot, gc.at[token_rows(s)], lsem.at[7]).wait()
     cot_in.finish()
     lax.fori_loop(0, 4, mask_cotangent, 0)
@@ -594,8 +654,7 @@
     o_finish()
     sum_one = seq_sum_start(lambda j: mm(attm[token_rows(j), :], wo[...], NN), sb_a, cr_a)
     seq_sum_across(sum_one, sb_a, cr_a, xr_a)
-    gather_1.forward(3)
-    gather_2.along_z()
+    gather_1.forward_far()
     branch = seq_sum_finish(sum_one, sb_a, cr_a, xr_a)
     o_mixed[...] = xs[token_rows(s), :].astype(F32) + branch + bias_out
     hat, _ = normalize(o_mixed[...])
@@ -604,7 +663,8 @@
     h2_in.start(h2.at[token_rows(s)])
     gather_2.forward(1)
     h2_in.forward()
-    gather_2.forward(2, 3)
+    gather_2.forward(2)
+    gather_2.relay()
     h2_in.finish()
     gather_1.finish()
 
@@ -620,6 +680,7 @@
         return carry
 
     lax.fori_loop(0, 4, widen, 0)
+    gather_2.forward_far()
 
     def column_products(left, right, out):
         def step(t, carry):
@@ -643,6 +704,7 @@
 
     sum_two = seq_sum_start(hidden_back, sb_a, cr_a)
     seq_sum_across(sum_two, sb_a, cr_a, xr_a)
+    reduce_2.across_last()
     column_products(h2, gp, g1)
     reduce_1.across_y()
     reduce_2.along_z(3)
@@ -664,6 +726,7 @@
     sum_three = seq_sum_start(lambda j: mm(act[token_rows(j), :], w2[...], NT), sb_b, cr_b)
     seq_sum_across(sum_three, sb_b, cr_b, xr_b)
     reduce_2.along_z(1)
+    reduce_1.across_last()
     gb_in.forward()
     gb_in.finish()
 
@@ -770,22 +833,24 @@
             heads += shr[slot]
         return total, heads
 
-    vectors(0, (0,), (y_peer,))
+    z_to_all, z_from_all = [z_dev(t) for t in (1, 2, 3)], [z_dev(-t) for t in (1, 2, 3)]
+    s_to_all, s_from_all = [(i, s_at(t)) for t in (1, 2, 3)], [(i, s_at(-t)) for t in (1, 2, 3)]
+    vectors(0, (1, 2, 3), z_to_all)
     seq_sum_across(sum_four, sb_a, cr_a, xr_a)
-    sms[1], shs[1] = vectors_sum(0, (0,), (y_peer,))
-    vectors(1, (1, 2, 3), [z_dev(t) for t in (1, 2, 3)])
-    reduce_1.pieces()
-    reduce_q.along_z(3)
-    sms[2], shs[2] = vectors_sum(1, (1, 2, 3), [z_dev(-t) for t in (1, 2, 3)])
-    vectors(2, (4, 5, 6), [(i, s_at(t)) for t in (1, 2, 3)])
+    reduce_q.along_z(3, 2)
+    reduce_q.relay()
     grad_h = seq_sum_finish(sum_four, sb_a, cr_a, xr_a)
     hat, inverse = normalize(xs[token_rows(s), :].astype(F32))
     o_gtok[...] += norm_back(grad_h, gain_one, hat, inverse)
-    reduce_q.along_z(2, 1)
-    reduce_q.relay()
+    reduce_q.along_z(1)
+    sms[1], shs[1] = vectors_sum(0, (1, 2, 3), z_from_all)
+    vectors(1, (4, 5, 6), s_to_all)
+    reduce_1.pieces()
+    sms[2], shs[2] = vectors_sum(1, (4, 5, 6), s_from_all)
+    vectors(2, (0,), (y_peer,))
     ro_pieces()
-    o_sm[...], o_sh[...] = vectors_sum(2, (4, 5, 6), [(i, s_at(-t)) for t in (1, 2, 3)])
     reduce_q.pieces()
+    o_sm[...], o_sh[...] = vectors_sum(2, (0,), (y_peer,))
     reduce_2.finish()
     reduce_1.finish()
     ro_finish()
@@ -852,6 +917,7 @@
     scratch += [pltpu.VMEM(shape, BF16) for shape in ((d, f_pad), (d, f_pad), (4 * LANES, d), (d, qw))]
     scratch += [pltpu.VMEM((n_z, h, w), BF16) for h, w in ((rb, f_pad), (rb, f_pad), (HEAD_ROWS, d), (rb, qw))]
     scratch += [pltpu.VMEM((n_z, h, w), BF16) for h, w in ((rb, f_pad), (rb, f_pad), (HEAD_ROWS, d), (rb, qw))]
+    scratch += [pltpu.VMEM((n_z, SLIVER, w), BF16) for w in (f_pad, f_pad)]
     for _ in range(2):
         scratch += [pltpu.VMEM((n, BLOCK, d), BF16) for n in (3, 2)] + [pltpu.VMEM((BLOCK, d), BF16)]
     scratch += [
@@ -862,8 +928,8 @@
         pltpu.VMEM((7, 16, d), F32),
         pltpu.VMEM((3, 32, LANES), F32),
         pltpu.VMEM((7, 32, LANES), F32),
-        pltpu.SemaphoreType.DMA((160,)),
-        pltpu.SemaphoreType.DMA((160,)),
+        pltpu.SemaphoreType.DMA((200,)),
+        pltpu.SemaphoreType.DMA((200,)),
         pltpu.SemaphoreType.DMA((8,)),
     ]
     mixed, grad_tokens, gq, go, g1, g2, small, by_head = pl.pallas_call(

time: 260 us -> 239 us (0.919)
  Pallas kernels: 232 us -> 210 us
    pallas_call x1, Pallas kernels: 232 us -> 210 us  [whole_layer(): pl.pallas_call(partial(layer_kernel, (slice_len, d, hd, f, qw, n_z)), out...]
where the time goes in v3:
time: 239 us; the launch traced here: 237 us
  Pallas kernels  210 us (88%)
  local copies, waits for them, and re-layouts  22.1 us (9%)
  other arithmetic  3.1 us (1%)
    pallas_call x1, Pallas kernels, whole_layer(): pl.pallas_call(partial(layer_kernel, (slice_len, d, hd, f, qw, n_z)), out...  210 us

profile of v3, /device:TPU:1, one launch (start us, length us, event | category | flops | bytes accessed | tf_op | source)
XLA Modules:
  0.0 236.9 jit_solution(1538996376751386447)
XLA Ops:
  0.6 0.0 copy-start.7
  1.3 0.7 pad_maximum_fusion
  2.0 0.8 dynamic-slice_convert_fusion
  2.8 0.6 pad.32.fb_ref
  3.4 0.1 copy.35
  3.5 0.0 copy-done.7
  3.5 0.7 pad.27.po
  4.2 1.2 reshape.51
  5.5 0.0 copy-start.2
  5.5 0.8 pad.28.p1
  6.3 0.3 copy-done.2
  6.6 0.3 reshape.52
  6.9 0.0 copy-start
  6.9 0.8 pad.29.p2
  7.7 0.4 copy-done
  8.1 0.8 pad.30.tok
  8.9 0.2 copy-done.5
  9.1 0.8 reshape.49
  9.9 0.2 copy.48
  10.1 0.4 reshape.50
  10.5 0.0 copy-start.1
  10.5 0.8 fusion.5.pq
  11.4 0.2 copy-done.1
  11.6 0.8 pad.31.cot
  12.4 210.2 %shard_map.169 = (f32[192,1152]{1,0:T(8,128)}, f32[192,1152]{1,0:T(8,128)}, bf16[4,48,896]{2,1,0:T(8,128)(2,1)}, bf16[48,1152]{1,0:T(8,128)(2,1)}, bf16[4,48,115...) custom-call(s32[1]{0:T(128)S(6)} %copy.51.off_ref, ...), custom_call_target="tpu_custom_call" | custom-call | tf_op jit(solution)/shard_map/pallas_call | solution.py:935
  222.5 1.5 slice_bitcast_fusion
  224.1 0.0 copy-start.10
  224.1 0.0 copy-start.9
  224.1 1.8 copy.44
  225.9 0.1 reshape.53
  226.0 0.1 constant_dynamic-slice_fusion
  226.1 0.1 constant_dynamic-slice_fusion.1
  226.1 0.6 slice_bitcast_fusion.2
  226.7 0.6 stack.3
  227.3 0.7 reshape.54
  228.0 0.0 copy-done.8
  228.0 0.7 slice_convert_fusion.1
  228.7 0.0 copy-done.6
  228.7 0.1 copy.39
  228.9 0.7 reshape.58
  229.6 0.5 copy.40
  230.1 2.2 reshape.55
  232.3 1.8 copy.43
  234.0 0.1 convert_bitcast_fusion
  234.1 0.2 copy.42
  234.3 1.2 reshape.57
  235.5 0.2 copy.41
  235.7 1.2 reshape.56
  (18 shorter events, 0.2 us)
Async XLA Ops:
  0.6 2.9 %copy-start.7 = (bf16[36,1152]{1,0:T(8,128)(2,1)S(1)}, bf16[36,1152]{1,0:T(8,128)(2,1)}, u32[]{:S(2)}) copy-start(bf16[36,1152]{1,0:T(8,128)(2,1)} %param.13) | copy-start | bytes 248836
  5.5 1.1 copy-start.2
  6.9 1.2 copy-start
  8.1 1.0 copy-start.5
  10.5 1.0 copy-start.1
  224.1 1.8 copy-start.10
  224.1 2.0 copy-start.9
  224.1 3.9 %copy-start.8 = (bf16[48,1152]{1,0:T(8,128)(2,1)S(1)}, bf16[48,1152]{1,0:T(8,128)(2,1)}, u32[]{:S(2)}) copy-start(bf16[48,1152]{1,0:T(8,128)(2,1)} %get-tuple-element.20) | copy-start | bytes 331780
  225.9 2.8 %copy-start.6 = (bf16[4,48,896]{2,1,0:T(8,128)(2,1)S(1)}, bf16[4,48,896]{2,1,0:T(8,128)(2,1)}, u32[]{:S(2)}) copy-start(bf16[4,48,896]{2,1,0:T(8,128)(2,1)} %get-tuple-element.19) | copy-start | bytes 1032196
  232.3 1.8 copy-start.3
  232.3 1.8 copy-start.4

commit v4 on v3

--- a/solution.py
+++ b/solution.py
@@ -43,7 +43,7 @@
     return tensor.transpose(1, 2, 0, 3).reshape(images_here, count, head_count * head_dim)
 
 
-VMEM_BYTES = 62 * 2**20
+VMEM_BYTES = 63 * 2**20
 MESH_IDS = pl.DeviceIdType.MESH
 F32 = jnp.float32
 BF16 = jnp.bfloat16
@@ -91,14 +91,54 @@
     return jnp.where(lanes < LANES - offset, first, second)
 
 
+def pack_lanes(parts, width, lanes):
+    tiles = {}
+    for n, part in enumerate(parts):
+        tile, offset = divmod(n * width, LANES)
+        if offset:
+            part = pltpu.roll(part, offset, 1)
+        ends = [(tile, lanes >= offset)]
+        if offset + width > LANES:
+            ends.append((tile + 1, lanes < offset + width - LANES))
+        for to, where in ends:
+            kept = jnp.where(where, part, 0.0)
+            tiles[to] = tiles[to] + kept if to in tiles else kept
+    return [tiles[to] for to in sorted(tiles)]
+
+
+class Tiles:
+    def __init__(self, ref, first, step, height):
+        self.ref, self.first, self.step, self.height = ref, first, step, height
+        self.wide = ref.shape[1] // LANES
+
+    def __getitem__(self, tile):
+        part, at = divmod(tile, self.wide)
+        row = self.first + part * self.step
+        return self.ref[row : row + self.height, at * LANES : (at + 1) * LANES]
+
+    def fill(self, source):
+        whole = self.wide * LANES
+        rows, wide = source.shape
+        for part in range(-(-wide // whole)):
+            row = self.first + part * self.step
+            width = min(whole, wide - part * whole)
+            self.ref[row + rows // 16 * 16 : row + self.height, :] = jnp.zeros(
+                (self.height - rows // 16 * 16, whole), F32
+            )
+            if width < whole:
+                last = width // LANES * LANES
+                self.ref[row : row + self.height, last : last + LANES] = jnp.zeros((self.height, LANES), F32)
+            self.ref[row : row + rows, 0:width] = source[:, part * whole : part * whole + width].astype(F32)
+
+
 def layer_kernel(
     dims,
-    off_ref, pq, po, p1, p2, tok, cot, fb_ref,
-    o_mixed, o_gtok, o_fq, o_fo, o_f1, o_f2, o_sm, o_sh,
+    off_ref, w_qkv, w_out, w_fc1, w_fc2, gains, biases, fc1_bias, tok, cot,
+    o_mixed, o_gtok, o_q, o_fo, o_1, o_2, o_fb, o_gains, o_biases,
     wq, wo, w1, w2, rq, ro, r1, r2, tmp,
-    xs, gc, h1, h2, act, gp, dg, qkv, attm, att_t, gatt, gpj, lse,
-    g1, g2, go, gq, y1, y2, yo, yq, z1, z2, zo, zq, s1, s2,
-    sb_a, cr_a, xr_a, sb_b, cr_b, xr_b, pf, prm, bh, sms, smr, shs, shr,
+    xs, gc, h1, h2, act, gp, dg, qkv, attm, att_t, lse,
+    g1, g2, gq, y1, y2, yo, yq, z1, z2, zo, zq, s1, s2,
+    sb_a, cr_a, xr_a, sb_b, cr_b, xr_b, pf, fb, prm, bh, sms, smr, shs, shr,
     ssem, rsem, lsem,
 ):
     slice_len, d, hd, f, qw, n_z = dims
@@ -173,7 +213,6 @@
     partners = [(i, s_at(t)) for t in (1, 2, 3)] + [z_dev(t) for t in range(1, n_z)] + [y_peer]
     for partner in partners:
         pl.semaphore_signal(barrier, inc=1, device_id=partner, device_id_type=MESH_IDS)
-    pl.semaphore_wait(barrier, len(partners))
 
     class Gather:
         def __init__(self, piece, recv, full, local_index):
@@ -181,16 +220,24 @@
             self.width = full.shape[1]
             self.sp, self.sz, self.sy, self.ss = take(4), take(n_z), take(n_z), take(n_z)
             self.local = local_index
+            self.started = []
 
         def pieces(self):
-            pltpu.make_async_copy(self.piece.at[s], self.recv.at[s], lsem.at[self.local]).start()
+            self.own_piece().start()
             for t in (1, 2, 3):
-                to = s_at(t)
-                send(self.piece.at[to], self.recv.at[s], self.sp + t, (i, to))
+                self.piece_to(t).start()
+
+        def own_piece(self):
+            return pltpu.make_async_copy(self.piece.at[s, 0:PIECE], self.recv.at[s], lsem.at[self.local])
+
+        def piece_to(self, t):
+            to = s_at(t)
+            return copy(self.piece.at[to, 0:PIECE], self.recv.at[s], self.sp + t, (i, to))
 
         def assemble(self):
-            pltpu.make_async_copy(self.piece.at[s], self.recv.at[s], lsem.at[self.local]).wait()
+            self.own_piece().wait()
             for t in (1, 2, 3):
+                self.piece_to(t).wait_send()
                 came = self.recv.at[s_at(-t)]
                 copy(came, came, self.sp + t, (i, s_at(-t))).wait_recv()
             part = rb // 4
@@ -211,12 +258,17 @@
             whole, part = self.block(z, 1 - y), self.sliver(z, 1 - y)
             copy(whole, whole, self.sy, y_peer, self.sy + z).wait_recv()
             for u in (1, 2, 3):
-                send(part, part, self.ss + u, z_to(near[u]), self.ss + z)
+                self.send(part, part, self.ss + u, z_to(near[u]), self.ss + z)
+
+        def send(self, src, dst, index, device, at):
+            made = copy(src, dst, index, device, at)
+            made.start()
+            self.started.append(made)
 
         def along_z(self):
             own = self.block(z, y)
             for u in (1, 2):
-                send(own, own, self.sz + u, z_to(near[u]), self.sz + z)
+                self.send(own, own, self.sz + u, z_to(near[u]), self.sz + z)
 
             @pl.when(middle)
             def _():
@@ -224,7 +276,7 @@
 
         def across_y(self):
             own = self.block(z, y)
-            send(own, own, self.sy, y_peer, self.sy + z)
+            self.send(own, own, self.sy, y_peer, self.sy + z)
 
         def forward(self, *steps):
             for u in steps:
@@ -257,6 +309,9 @@
                 copy(came, came, self.ss, z_to(zb), self.ss + zb).wait_recv()
 
         def sent(self):
+            for made in self.started:
+                made.wait_send()
+
             @pl.when(middle)
             def _():
                 own, came = self.block(z, y), self.block(near[3], y)
@@ -267,13 +322,15 @@
                 came = self.most(near[u], y)
                 copy(came, came, self.sy + u, y_peer, self.sy + near[u]).wait_send()
 
-    gather_q = Gather(pq, rq, wq, 0)
-    gather_1 = Gather(p1, r1, w1, 1)
-    gather_2 = Gather(p2, r2, w2, 2)
+    gather_q = Gather(yq, rq, wq, 0)
+    gather_1 = Gather(y1, r1, w1, 1)
+    gather_2 = Gather(y2, r2, w2, 2)
     o_piece, o_z, o_y = take(), take(n_z), take(n_z)
 
     def head_block(array, t):
         return array.at[pl.ds(pl.multiple_of(z_at(-t) * LANES, LANES), HEAD_ROWS)]
+
+    po = yo.at[0, 0:PIECE]
 
     def o_start():
         @pl.when(cy)
@@ -285,6 +342,10 @@
             copy(po, ro.at[c], o_piece, core_peer).start()
 
     def o_assemble():
+        @pl.when(jnp.logical_not(cy))
+        def _():
+            copy(po, ro.at[c], o_piece, core_peer).wait_send()
+
         for h in range(4):
             wo[h * LANES + HEAD_ROWS : (h + 1) * LANES, :] = jnp.zeros((LANES - HEAD_ROWS, d), BF16)
 
@@ -320,10 +381,6 @@
                 copy(came, came, o_y + t, y_peer).wait_recv()
 
     def o_sent():
-        @pl.when(jnp.logical_not(cy))
-        def _():
-            copy(po, ro.at[c], o_piece, core_peer).wait_send()
-
         @pl.when(cy)
         def _():
             mine = head_block(wo, 0)
@@ -404,6 +461,9 @@
             self.most = rb if zs is None else rb - SLIVER
             self.width = grad.shape[1]
             self.sy, self.sz, self.sp, self.ss = take(n_z), take(n_z), take(4), take(n_z)
+
+        def kept(self, j):
+            return w1.at[pl.ds(pl.multiple_of(self.out + j * PIECE, 16), PIECE), 0 : self.width]
 
         def at(self, zb, side):
             return img_rows(zb * 2 + side)
@@ -476,11 +536,11 @@
             part = rb // 4
             for j in range(4):
                 self.fs[j] = tmp[part * j : part * j + PIECE, 0 : self.width].astype(BF16)
-            pltpu.make_async_copy(self.fs.at[s], self.out.at[s], lsem.at[4]).start()
+            pltpu.make_async_copy(self.fs.at[s], self.kept(s), lsem.at[4]).start()
             for t in (1, 2, 3):
                 to = s_at(t)
-                send(self.fs.at[to], self.out.at[s], self.sp + t, (i, to))
-            pltpu.make_async_copy(self.fs.at[s], self.out.at[s], lsem.at[4]).wait()
+                send(self.fs.at[to], self.kept(s), self.sp + t, (i, to))
+            pltpu.make_async_copy(self.fs.at[s], self.kept(s), lsem.at[4]).wait()
 
         def sent(self):
             @pl.when(middle)
@@ -493,12 +553,49 @@
 
         def finish(self):
             for t in (1, 2, 3):
-                came = self.out.at[s_at(-t)]
+                came = self.kept(s_at(-t))
                 copy(came, came, self.sp + t, (i, s_at(-t))).wait_recv()
 
-    reduce_2 = Reduce(g2, y2, z2, s2, r2, o_f2)
-    reduce_1 = Reduce(g1, y1, z1, s1, r1, o_f1)
-    reduce_q = Reduce(gq, yq, zq, None, rq, o_fq)
+        def piece_tiles(self, j):
+            row = self.out + j * PIECE
+            return [
+                w1[row : row + PIECE, t * LANES : (t + 1) * LANES].astype(F32) for t in range(self.width // LANES)
+            ]
+
+        def publish(self, tiles, out):
+            for t, tile in enumerate(tiles):
+                width = min(LANES, out.shape[1] - t * LANES)
+                out[:, t * LANES : t * LANES + width] = tile[0:own, 0:width]
+
+        def publish_wide(self, out):
+            tiles = {}
+            for j in range(4):
+                tile, offset = divmod(j * f, LANES)
+                for t, part in enumerate(self.piece_tiles(j)):
+                    if offset:
+                        part = pltpu.roll(part, offset, 1)
+                    for to, where in ((tile + t, piece_lanes >= offset), (tile + t + 1, piece_lanes < offset)):
+                        if to * LANES < 4 * f:
+                            kept = jnp.where(where, part, 0.0)
+                            tiles[to] = tiles[to] + kept if to in tiles else kept
+            self.publish([tiles[to] for to in sorted(tiles)], out)
+
+        def publish_heads(self, out):
+            pieces = [self.piece_tiles(j) for j in range(4)]
+            tiles = []
+            for kind in range(3):
+                parts = []
+                for head in range(d // hd):
+                    which, to = divmod(head, 4)
+                    part = lane_window(pieces[2 * (to % 2) + to // 2], (4 * kind + which) * hd, hd, piece_lanes)
+                    parts.append(jnp.where(piece_lanes < hd, part, 0.0))
+                tiles += pack_lanes(parts, hd, piece_lanes)
+            self.publish(tiles, out)
+
+    reduce_2 = Reduce(g2, y2, z2, s2, r2, 0)
+    reduce_1 = Reduce(g1, y1, z1, s1, r1, 4 * PIECE)
+    reduce_q = Reduce(gq, yq, zq, None, rq, 8 * PIECE)
+    go = wo
     ro_y, ro_z, ro_p = take(n_z), take(n_z), take()
 
     def ro_across_y():
@@ -550,15 +647,59 @@
         position = j * slice_len + t
         return (t < slice_len) & (position >= off_ref[0]) & (position < off_ref[0] + VALID)
 
+    def padded(rows_in):
+        pf[0, BLOCK - 16 : BLOCK, :] = jnp.zeros((16, d), F32)
+        pf[0, 0:slice_len, :] = rows_in[0]
+        return pf[0]
+
     tokens_in, cot_in = TokenGather(xs), TokenGather(gc)
+    piece_lanes = lane_ids(PIECE)
+    three = [Tiles(dg, PIECE * n, PIECE, PIECE) for n in range(3)]
+    for n in range(3):
+        three[n].fill(w_qkv.at[:, n * d : (n + 1) * d])
+    small = Tiles(dg, 3 * PIECE, PIECE, PIECE)
+    dg[3 * PIECE : 3 * PIECE + LANES, 0:LANES] = jnp.zeros((LANES, LANES), F32)
+    dg[3 * PIECE : 3 * PIECE + 2, 0:own] = gains[...].astype(F32)
+    dg[3 * PIECE + 2 : 3 * PIECE + 8, 0:own] = biases[...].astype(F32)
+    dg[3 * PIECE : 3 * PIECE + LANES, 0:LANES] = dg[3 * PIECE : 3 * PIECE + LANES, 0:LANES].T
+    for to in range(4):
+        parts = []
+        for n in range(12):
+            kind, which = divmod(n, 4)
+            head = 4 * which + 2 * (to % 2) + to // 2
+            part = lane_window(three[kind], head * hd, hd, piece_lanes)
+            parts.append(jnp.where(piece_lanes < hd, part, 0.0))
+        tiles = pack_lanes(parts, hd, piece_lanes)
+        tiles[-1] = tiles[-1] + pltpu.roll(small[0], 12 * hd % LANES, 1)
+        for at, tile in enumerate(tiles):
+            yq[to, 0:PIECE, at * LANES : (at + 1) * LANES] = tile.astype(BF16)
+    pl.semaphore_wait(barrier, len(partners))
     gather_q.pieces()
-    pltpu.make_async_copy(tok, xs.at[token_rows(s)], lsem.at[6]).start()
-    pltpu.make_async_copy(cot, gc.at[token_rows(s)], lsem.at[7]).start()
-    tokens_in.start(tok)
+    pf[0, BLOCK - 16 : BLOCK, :] = jnp.zeros((16, d), F32)
+    pf[0, 0:slice_len, :] = tok[0].astype(F32)
+    xs[token_rows(s), :] = pf[0].astype(BF16)
+    tokens_in.start(xs.at[token_rows(s)])
+    out_rows = Tiles(dg, 12 * PIECE, PIECE, PIECE)
+    out_rows.fill(w_out)
+    for at in range(d // LANES):
+        yo[0, 0:PIECE, at * LANES : (at + 1) * LANES] = out_rows[at].astype(BF16)
     o_start()
-    gather_1.pieces()
-    gather_2.pieces()
-    cot_in.start(cot)
+    for weights, first, pieces in ((w_fc1, 4, y1), (w_fc2, 8, y2)):
+        wide = Tiles(dg, first * PIECE, PIECE, PIECE)
+        wide.fill(weights)
+        for to in range(4):
+            for at in range(w1.shape[1] // LANES):
+                start = to * f + at * LANES
+                width = min(LANES, f - at * LANES)
+                part = lane_window(wide, start, width, piece_lanes)
+                if width < LANES:
+                    part = jnp.where(piece_lanes < width, part, 0.0)
+                pieces[to, 0:PIECE, at * LANES : (at + 1) * LANES] = part.astype(BF16)
+        (gather_1 if first == 4 else gather_2).pieces()
+    pf[1, BLOCK - 16 : BLOCK, :] = jnp.zeros((16, d), F32)
+    pf[1, 0:slice_len, :] = cot[0].astype(F32)
+    gc[token_rows(s), :] = jnp.where(real_rows(s, d), pf[1], 0.0).astype(BF16)
+    cot_in.start(gc.at[token_rows(s)])
     sms[0] = jnp.zeros(sms.shape[1:], F32)
     shs[0] = jnp.zeros(shs.shape[1:], F32)
     tmp[...] = jnp.zeros(tmp.shape, F32)
@@ -581,13 +722,7 @@
     o_forward()
     gather_2.across_y()
     cot_in.forward()
-    pltpu.make_async_copy(tok, xs.at[token_rows(s)], lsem.at[6]).wait()
     tokens_in.finish()
-    def mask_cotangent(j, carry):
-        kept = gc[token_rows(j), :].astype(F32)
-        gc[token_rows(j), :] = jnp.where(real_rows(j, d), kept, 0.0).astype(BF16)
-        return carry
-
     gather_q.finish()
 
     packed = 3 * 4 * hd
@@ -646,9 +781,17 @@
     gather_1.relay()
     gather_2.slivers()
 
-    pltpu.make_async_copy(cot, gc.at[token_rows(s)], lsem.at[7]).wait()
     cot_in.finish()
-    lax.fori_loop(0, 4, mask_cotangent, 0)
+    bias_parts = Tiles(dg, 14 * PIECE, 8, 8)
+    bias_parts.fill(fc1_bias)
+    row_lanes = lane_ids(8)
+    for at in range(w1.shape[1] // LANES):
+        width = min(LANES, f - at * LANES)
+        mine = jnp.zeros((8, LANES), F32)
+        for to in range(4):
+            part = lane_window(bias_parts, to * f + at * LANES, width, row_lanes)
+            mine = jnp.where(s == to, part, mine)
+        fb[:, at * LANES : (at + 1) * LANES] = jnp.where(row_lanes < width, mine, 0.0)[0:1]
 
     gather_1.forward(2)
     o_finish()
@@ -656,8 +799,9 @@
     seq_sum_across(sum_one, sb_a, cr_a, xr_a)
     gather_1.forward_far()
     branch = seq_sum_finish(sum_one, sb_a, cr_a, xr_a)
-    o_mixed[...] = xs[token_rows(s), :].astype(F32) + branch + bias_out
-    hat, _ = normalize(o_mixed[...])
+    middle_rows = xs[token_rows(s), :].astype(F32) + branch + bias_out
+    o_mixed[0] = middle_rows[0:slice_len]
+    hat, _ = normalize(middle_rows)
     h2[token_rows(s), :] = (hat * gain_two + shift_two).astype(BF16)
     h2_in = TokenGather(h2)
     h2_in.start(h2.at[token_rows(s)])
@@ -671,7 +815,7 @@
     slope = (2.0 / 3.141592653589793) ** 0.5
 
     def widen(j, carry):
-        pre = mm(h2[token_rows(j), :], w1[...], NN) + fb_ref[...]
+        pre = mm(h2[token_rows(j), :], w1[...], NN) + fb[...]
         square = pre * pre
         curve = jnp.tanh(slope * pre * (1.0 + 0.044715 * square))
         half = 0.5 + 0.5 * curve
@@ -702,6 +846,7 @@
         sms[0, pl.ds(8 + s, 1), :] += column
         return mm(low, w1[...], NT)
 
+    gather_1.sent()
     sum_two = seq_sum_start(hidden_back, sb_a, cr_a)
     seq_sum_across(sum_two, sb_a, cr_a, xr_a)
     reduce_2.across_last()
@@ -710,10 +855,10 @@
     reduce_2.along_z(3)
     reduce_2.along_z(2)
     grad_h = seq_sum_finish(sum_two, sb_a, cr_a, xr_a)
-    hat, inverse = normalize(o_mixed[...])
+    hat, inverse = normalize(padded(o_mixed))
     kept = gc[token_rows(s), :].astype(F32)
     grad_x = kept + norm_back(grad_h, gain_two, hat, inverse)
-    o_gtok[...] = grad_x
+    o_gtok[0] = grad_x[0:slice_len]
     low = grad_x.astype(BF16)
     sms[0, 1:2, :] = jnp.sum(grad_h * hat, 0, keepdims=True)
     sms[0, 4:5, :] = jnp.sum(grad_h, 0, keepdims=True)
@@ -731,12 +876,12 @@
     gb_in.finish()
 
     def attended_back(j, carry):
-        wide = mm(gc[token_rows(j), :], wo[...], NT).astype(BF16)
-        for head in range(4):
-            gatt[head, token_rows(j), :] = wide[:, head * LANES : (head + 1) * LANES]
+        attm[token_rows(j), :] = mm(gc[token_rows(j), :], wo[...], NT).astype(BF16)
         return carry
 
     lax.fori_loop(0, 4, attended_back, 0)
+
+    o_sent()
 
     def out_products(head, carry):
         at = pl.ds(pl.multiple_of(head * LANES, LANES), LANES)
@@ -747,7 +892,7 @@
     ro_across_y()
     reduce_2.relay()
     branch = seq_sum_finish(sum_three, sb_b, cr_b, xr_b)
-    o_mixed[...] = jnp.where(real_rows(s, d), o_mixed[...] + branch + bias_two, 0.0)
+    o_mixed[0] = jnp.where(real_rows(s, d), padded(o_mixed) + branch + bias_two, 0.0)[0:slice_len]
 
     wide_lanes = lane_ids(rows)
     chunk_lanes = lane_ids(chunk)
@@ -758,7 +903,7 @@
         grad_q = []
         for part in range(rows // chunk):
             at = slice(part * chunk, (part + 1) * chunk)
-            query, grad_out = qkv[head, at, :], gatt[head, at, :]
+            query, grad_out = qkv[head, at, :], attm[at, pl.ds(pl.multiple_of(head * LANES, LANES), LANES)]
             scores = mm(qkv[4 + head], query, NT)
             probs = jnp.exp(scores * scale - lse[head, :, at])
             grad_p = mm(qkv[8 + head], grad_out, NT)
@@ -785,20 +930,11 @@
     reduce_1.along_z(1)
     reduce_1.relay()
 
+    gpj = h2.at[:, 0:qw]
+
     def pack(j, carry):
-        tiles = [None] * (qw // LANES)
-        for n in range(12):
-            tile, offset = divmod(n * hd, LANES)
-            part = qkv[n, token_rows(j), :].astype(F32)
-            if offset:
-                part = pltpu.roll(part, offset, 1)
-            ends = [(tile, lanes >= offset)]
-            if offset + hd > LANES:
-                ends.append((tile + 1, lanes < offset + hd - LANES))
-            for to, where in ends:
-                kept = jnp.where(where, part, 0.0)
-                tiles[to] = kept if tiles[to] is None else tiles[to] + kept
-        for to, tile in enumerate(tiles):
+        parts = [qkv[n, token_rows(j), :].astype(F32) for n in range(12)]
+        for to, tile in enumerate(pack_lanes(parts, hd, lanes)):
             gpj[token_rows(j), LANES * to : LANES * (to + 1)] = tile.astype(BF16)
         return carry
 
@@ -841,25 +977,65 @@
     reduce_q.relay()
     grad_h = seq_sum_finish(sum_four, sb_a, cr_a, xr_a)
     hat, inverse = normalize(xs[token_rows(s), :].astype(F32))
-    o_gtok[...] += norm_back(grad_h, gain_one, hat, inverse)
+    o_gtok[0] = (padded(o_gtok) + norm_back(grad_h, gain_one, hat, inverse))[0:slice_len]
     reduce_q.along_z(1)
     sms[1], shs[1] = vectors_sum(0, (1, 2, 3), z_from_all)
     vectors(1, (4, 5, 6), s_to_all)
     reduce_1.pieces()
+    reduce_2.finish()
+    reduce_2.publish_wide(o_2)
     sms[2], shs[2] = vectors_sum(1, (4, 5, 6), s_from_all)
     vectors(2, (0,), (y_peer,))
     ro_pieces()
     reduce_q.pieces()
-    o_sm[...], o_sh[...] = vectors_sum(2, (0,), (y_peer,))
-    reduce_2.finish()
     reduce_1.finish()
+    reduce_1.publish_wide(o_1)
+    summed_rows, by_head = vectors_sum(2, (0,), (y_peer,))
+    mine = smr.at[1]
+    for to, row in enumerate((0, 1, 2, None, None, 3, 4, 5)):
+        if row is not None:
+            mine[to : to + 1, :] = summed_rows[row : row + 1, :]
+    for which in range(2):
+        heads = [by_head[16 * which + head : 16 * which + head + 1, :] for head in range(d // hd)]
+        for to, tile in enumerate(pack_lanes(heads, hd, one_lane)):
+            mine[3 + which : 4 + which, to * LANES : (to + 1) * LANES] = tile
+    start = (i * 4 + s) * own
+    turned = pltpu.roll(mine[0:8, :], lax.rem(d - start, d), 1)
+    o_gains[...] = turned[0:2, 0:own]
+    o_biases[...] = turned[2:8, 0:own]
+    spread = {}
+    for j in range(4):
+        tile, offset = divmod(j * f, LANES)
+        for t in range(w1.shape[1] // LANES):
+            part = summed_rows[8 + j : 9 + j, t * LANES : (t + 1) * LANES]
+            if offset:
+                part = pltpu.roll(part, offset, 1)
+            for to, where in ((tile + t, one_lane >= offset), (tile + t + 1, one_lane < offset)):
+                if to * LANES < 4 * f:
+                    kept = jnp.where(where, part, 0.0)
+                    spread[to] = spread[to] + kept if to in spread else kept
+    for to, tile in spread.items():
+        width = min(LANES, 4 * f - to * LANES)
+        o_fb[:, to * LANES : to * LANES + width] = tile[:, 0:width]
     ro_finish()
-    o_sent()
     reduce_q.finish()
-    for part in (gather_q, gather_1, gather_2, reduce_q, reduce_1, reduce_2):
+    reduce_q.publish_heads(o_q)
+    for part in (gather_q, gather_2, reduce_q, reduce_1, reduce_2):
         part.sent()
     for made in sends:
         made.wait_send()
+
+
+def hand_over(mixed, tokens, g_qkv, g_1, g_2, g_out, g_gains, g_biases, *outs):
+    o_mixed, o_tokens, o_qkv, o_1, o_2, o_out, o_gains, o_biases = outs
+    o_qkv[...] = g_qkv[...]
+    o_1[...] = g_1[...]
+    o_2[...] = g_2[...]
+    o_mixed[:, 0, :] = mixed[0]
+    o_tokens[:, 0, :] = tokens[0]
+    o_out[...] = g_out[0 : o_out.shape[0], :].astype(F32)
+    o_gains[...] = g_gains[...]
+    o_biases[...] = g_biases[...]
 
 
 def whole_layer(tokens, offsets, w_qkv, w_out, w_fc1, w_fc2, gains, biases, fc1_bias, cotangent):
@@ -873,30 +1049,19 @@
     n_z = lax.axis_size("img") // 2
     rb = own * 4
     rows = 4 * BLOCK
-    seq = lax.axis_index("seq")
-
-    def grow(array, *shape):
-        return jnp.pad(array, [(0, to - at) for at, to in zip(array.shape, shape, strict=True)])
-
-    heads = w_qkv.reshape(own, 3, n_z, 2, 2, hd).transpose(4, 3, 0, 1, 2, 5).reshape(4, own, packed)
-    vectors = jnp.broadcast_to(jnp.concatenate([gains, biases], 1)[None], (4, own, 8))
-    pq = grow(jnp.concatenate([heads, vectors], 2), 4, PIECE, qw)
-    p1, p2 = (grow(w.reshape(own, 4, f).transpose(1, 0, 2), 4, PIECE, f_pad) for w in (w_fc1, w_fc2))
-    po = grow(w_out, PIECE, d)
-    tok, cot = grow(tokens[0], BLOCK, d), grow(cotangent[0], BLOCK, d)
-    fb = grow(lax.dynamic_slice(fc1_bias.astype(F32), (seq * f,), (f,))[None], 1, f_pad)
 
     hbm = pl.BlockSpec(memory_space=pl.ANY)
     vmem = pl.BlockSpec(memory_space=pltpu.VMEM)
     outs = [
-        ((BLOCK, d), F32, vmem),
-        ((BLOCK, d), F32, vmem),
-        ((4, PIECE, qw), BF16, hbm),
+        ((1, slice_len, d), F32, vmem),
+        ((1, slice_len, d), F32, vmem),
+        ((own, 3 * d), F32, vmem),
         ((PIECE, d), BF16, hbm),
-        ((4, PIECE, f_pad), BF16, hbm),
-        ((4, PIECE, f_pad), BF16, hbm),
-        ((16, d), F32, vmem),
-        ((32, LANES), F32, vmem),
+        ((own, wide), F32, vmem),
+        ((own, wide), F32, vmem),
+        ((1, wide), F32, vmem),
+        ((2, own), F32, vmem),
+        ((6, own), F32, vmem),
     ]
     low = [
         (d, qw), (4 * LANES, d), (d, f_pad), (d, f_pad),
@@ -910,11 +1075,9 @@
         pltpu.VMEM((12, rows, LANES), BF16),
         pltpu.VMEM((rows, 4 * LANES), BF16),
         pltpu.VMEM((4, LANES, rows), BF16),
-        pltpu.VMEM((4, rows, LANES), BF16),
-        pltpu.VMEM((rows, qw), BF16),
         pltpu.VMEM((4, 1, rows), F32),
     ]
-    scratch += [pltpu.VMEM(shape, BF16) for shape in ((d, f_pad), (d, f_pad), (4 * LANES, d), (d, qw))]
+    scratch += [pltpu.VMEM(shape, BF16) for shape in ((d, f_pad), (d, f_pad), (d, qw))]
     scratch += [pltpu.VMEM((n_z, h, w), BF16) for h, w in ((rb, f_pad), (rb, f_pad), (HEAD_ROWS, d), (rb, qw))]
     scratch += [pltpu.VMEM((n_z, h, w), BF16) for h, w in ((rb, f_pad), (rb, f_pad), (HEAD_ROWS, d), (rb, qw))]
     scratch += [pltpu.VMEM((n_z, SLIVER, w), BF16) for w in (f_pad, f_pad)]
@@ -922,6 +1085,7 @@
         scratch += [pltpu.VMEM((n, BLOCK, d), BF16) for n in (3, 2)] + [pltpu.VMEM((BLOCK, d), BF16)]
     scratch += [
         pltpu.VMEM((2, BLOCK, d), F32),
+        pltpu.VMEM((1, f_pad), F32),
         pltpu.VMEM((8, d), F32),
         pltpu.VMEM((2, 16, LANES), F32),
         pltpu.VMEM((3, 16, d), F32),
@@ -932,34 +1096,28 @@
         pltpu.SemaphoreType.DMA((200,)),
         pltpu.SemaphoreType.DMA((8,)),
     ]
-    mixed, grad_tokens, gq, go, g1, g2, small, by_head = pl.pallas_call(
+    mixed, grad_tokens, gq, go, g1, g2, g_fb, g_gains, g_biases = pl.pallas_call(
         partial(layer_kernel, (slice_len, d, hd, f, qw, n_z)),
         out_shape=[jax.ShapeDtypeStruct(shape, kind) for shape, kind, _ in outs],
-        in_specs=[pl.BlockSpec(memory_space=pltpu.SMEM)] + [hbm] * 6 + [vmem],
+        in_specs=[pl.BlockSpec(memory_space=pltpu.SMEM)] + [vmem] * 9,
         out_specs=[spec for _, _, spec in outs],
         scratch_shapes=scratch,
         compiler_params=pltpu.CompilerParams(
             collective_id=0, has_side_effects=True, vmem_limit_bytes=VMEM_BYTES
         ),
-    )(offsets, pq, po, p1, p2, tok, cot, fb)
-
-    mixed, grad_tokens = mixed[None, :slice_len], grad_tokens[None, :slice_len]
-    grad_qkv = (
-        gq[:, :own, :packed]
-        .reshape(2, 2, own, 3, n_z, hd)
-        .transpose(2, 3, 4, 1, 0, 5)
-        .reshape(own, 3 * d)
-        .astype(F32)
-    )
-    grad_out = go[:own].astype(F32)
-    grad_fc1, grad_fc2 = (g[:, :own, :f].transpose(1, 0, 2).reshape(own, wide).astype(F32) for g in (g1, g2))
-    start = (lax.axis_index("img") * 4 + seq) * own
-    mine = lax.dynamic_slice(small[:8], (0, start), (8, own))
-    query_value = lax.dynamic_slice(by_head[:, :hd].reshape(2, d), (0, start), (2, own))
-    grad_gains = mine[:2].T
-    grad_biases = jnp.stack([mine[2], query_value[0], query_value[1], mine[3], mine[4], mine[5]], 1)
-    grad_fc1_bias = small[8:12, :f].reshape(wide)
-    return mixed, grad_tokens, grad_qkv, grad_out, grad_fc1, grad_fc2, grad_gains, grad_biases, grad_fc1_bias
+    )(offsets, w_qkv, w_out, w_fc1, w_fc2, gains.T, biases.T, fc1_bias[None], tokens, cotangent)
+
+    rows_out = jax.ShapeDtypeStruct((slice_len, 1, d), F32)
+    same = [jax.ShapeDtypeStruct(made.shape, F32) for made in (gq, g1, g2)]
+    rest = [jax.ShapeDtypeStruct(shape, F32) for shape in ((own, d), (2, own), (6, own))]
+    mixed, grad_tokens, gq, g1, g2, go, g_gains, g_biases = pl.pallas_call(
+        hand_over,
+        out_shape=[rows_out, rows_out, *same, *rest],
+        in_specs=[vmem] * 8,
+        out_specs=[vmem] * 8,
+    )(mixed, grad_tokens, gq, g1, g2, go, g_gains, g_biases)
+    mixed, grad_tokens = mixed.reshape(tokens.shape), grad_tokens.reshape(tokens.shape)
+    return mixed, grad_tokens, gq, go, g1, g2, g_gains.T, g_biases.T, g_fb.reshape(wide)
 
 
 def local(tokens, offsets, w_qkv, w_out, w_fc1, w_fc2, gains, biases, fc1_bias, cotangent):

time: 239 us -> 222 us (0.929)
  local copies, waits for them, and re-layouts: 22.1 us -> 2.03 us
  Pallas kernels: 210 us -> 216 us
  other arithmetic: 3.1 us -> 0.65 us
    convert_element_type x8 -> x0, local copies, waits for them, and re-layouts: 6.27 us -> none  [the longest x4 3.49 us: whole_layer(): grad_qkv = gq[:, :own, :packed].reshape(2, 2, own, 3, n_z, hd).transpose(...]
    pad x6 -> x0, local copies, waits for them, and re-layouts: 4.45 us -> none  [grow(): jnp.pad(array, [(0, to - at) for at, to in zip(array.shape, shape, strict...]
    pallas_call x0 -> x1, Pallas kernels: none -> 3.97 us  [whole_layer(): pl.pallas_call(hand_over, out_shape=[rows_out, rows_out, *same, *rest], i...]
    unnamed x24 -> x2, local copies, waits for them, and re-layouts: 4.63 us -> 0.71 us
    reshape x10 -> x0, local copies, waits for them, and re-layouts: 3.78 us -> none  [the longest x4 1.62 us: whole_layer(): w.reshape(own, 4, f).transpose(1, 0, 2)]
where the time goes in v4:
time: 222 us; the launch traced here: 220 us
  Pallas kernels  216 us (97%)
    pallas_call x1, Pallas kernels, whole_layer(): pl.pallas_call(partial(layer_kernel, (slice_len, d, hd, f, qw, n_z)), out...  212 us

profile of v4, /device:TPU:1, one launch (start us, length us, event | category | flops | bytes accessed | tf_op | source)
XLA Modules:
  0.0 220.2 jit_solution(6264909903282698526)
XLA Ops:
  0.6 1.3 broadcast_in_dim.3.fc1_bias
  2.6 212.2 %shard_map.169 = (f32[1,183,1152]{2,1,0:T(8,128)}, f32[1,183,1152]{2,1,0:T(8,128)}, f32[36,3456]{1,0:T(8,128)}, bf16[48,1152]{1,0:T(8,128)(2,1)}, f32[36,4304]{1...) custom-call(s32[1]{0:T(128)S(6)} %copy.19.off_ref, ...), custom_call_target="tpu_custom_call" | custom-call | tf_op jit(solution)/shard_map/pallas_call | solution.py:1099
  214.8 4.0 %shard_map.170 = (f32[183,1,1152]{2,1,0:T(1,128)}, f32[183,1,1152]{2,1,0:T(1,128)}, f32[36,3456]{1,0:T(8,128)}, f32[36,4304]{1,0:T(8,128)}, f32[36,4304]{1,0:T(8...) custom-call(f32[1,183,1152]{2,1,0:T(8,128)} %get-tuple-element.26.mixed, ...), custom_call_target="tpu_custom_call" | custom-call | tf_op jit(solution)/shard_map/pallas_call | solution.py:1113
  218.8 0.0 copy-start
  218.8 0.7 copy-done
  219.5 0.7 reduce
Async XLA Ops:
  218.8 0.7 copy-start

commit v5 on v4

--- a/solution.py
+++ b/solution.py
@@ -408,52 +408,75 @@
             copy(across, across, self.sx, x_peer).wait_recv()
             copy(across, across, self.sd, core_peer).start()
 
-        def finish(self):
-            for index, j in ((self.sc, x * 2 + 1 - c), (self.sd, (1 - x) * 2 + 1 - c)):
-                copy(self.at(j), self.at(j), index, core_peer).wait_recv()
+        def take_step(self, t):
+            @pl.when(t == 1)
+            def _():
+                came = self.at(x * 2 + 1 - c)
+                copy(came, came, self.sc, core_peer).wait_recv()
+
+            pl.when(t == 2)(self.forward)
+
+            @pl.when(t == 3)
+            def _():
+                came = self.at((1 - x) * 2 + 1 - c)
+                copy(came, came, self.sd, core_peer).wait_recv()
+
+        def sent(self):
             copy(self.own, self.at(s), self.sx, x_peer).wait_send()
             copy(self.own, self.at(s), self.sc, core_peer).wait_send()
             across = self.at((1 - x) * 2 + c)
             copy(across, across, self.sd, core_peer).wait_send()
 
-    def seq_sum_start(partial, sb, cr):
-        first = take(2)
-        last = take()
-
-        def step(t, carry):
-            away = t < 2
-            j = jnp.where(away, 2 * t + 1 - c, jnp.where(t == 2, 2 * (1 - x) + c, s))
-            part = partial(j)
-
-            @pl.when(away)
-            def _():
-                sb[t] = part.astype(BF16)
-                copy(sb.at[t], cr.at[t], first + t, core_peer).start()
-
-            @pl.when(t >= 2)
-            def _():
-                pf[t - 2] = part
-
-            return carry
-
-        lax.fori_loop(0, 4, step, 0)
-        return first, last
-
-    def seq_sum_across(handle, sb, cr, xr):
-        first, last = handle
-        there = 1 - x
-        copy(cr.at[there], cr.at[there], first + there, core_peer).wait_recv()
-        sb[2] = (pf[0] + cr[there].astype(F32)).astype(BF16)
-        copy(sb.at[2], xr, last, x_peer).start()
-
-    def seq_sum_finish(handle, sb, cr, xr):
-        first, last = handle
-        copy(cr.at[x], cr.at[x], first + x, core_peer).wait_recv()
-        copy(xr, xr, last, x_peer).wait_recv()
-        for t in range(2):
-            copy(sb.at[t], cr.at[t], first + t, core_peer).wait_send()
-        copy(sb.at[2], xr, last, x_peer).wait_send()
-        return pf[1] + cr[x].astype(F32) + xr[...].astype(F32)
+        def finish(self):
+            for index, j in ((self.sc, x * 2 + 1 - c), (self.sd, (1 - x) * 2 + 1 - c)):
+                copy(self.at(j), self.at(j), index, core_peer).wait_recv()
+            self.sent()
+
+    class SeqSum:
+        def __init__(self, partial, sb, cr, xr):
+            self.partial, self.sb, self.cr, self.xr = partial, sb, cr, xr
+            self.first, self.last = take(2), take()
+
+        def to_core(self, slot):
+            return copy(self.sb.at[slot], self.cr.at[slot], self.first + slot, core_peer)
+
+        def to_chip(self):
+            return copy(self.sb.at[2], self.xr, self.last, x_peer)
+
+        def run(self, low=0, high=4):
+            partial = self.partial
+
+            def step(t, carry):
+                away, slot = lax.rem(t, 2) == 0, lax.div(t, 2)
+                if low < 2 < high:
+                    pl.when(t == 2)(self.across)
+                part = partial(jnp.where(t < 2, 1 - x, x) * 2 + jnp.where(away, 1 - c, c))
+
+                @pl.when(away)
+                def _():
+                    self.sb[slot] = part.astype(BF16)
+                    self.to_core(slot).start()
+
+                @pl.when(jnp.logical_not(away))
+                def _():
+                    pf[slot] = part
+
+                return carry
+
+            lax.fori_loop(low, high, step, 0)
+
+        def across(self):
+            copy(self.cr.at[0], self.cr.at[0], self.first, core_peer).wait_recv()
+            self.sb[2] = (pf[0] + self.cr[0].astype(F32)).astype(BF16)
+            self.to_chip().start()
+
+        def finish(self):
+            copy(self.cr.at[1], self.cr.at[1], self.first + 1, core_peer).wait_recv()
+            copy(self.xr, self.xr, self.last, x_peer).wait_recv()
+            for slot in range(2):
+                self.to_core(slot).wait_send()
+            self.to_chip().wait_send()
+            return pf[1] + self.cr[1].astype(F32) + self.xr[...].astype(F32)
 
     class Reduce:
         def __init__(self, grad, yr, zr, zs, fs, out):
@@ -641,6 +664,9 @@
             for t in range(n_z):
                 copy(head_block(go, -t), yo.at[t], ro_y + t, y_peer).wait_send()
             copy(o_fo, o_fo, ro_p, core_peer).wait_recv()
+
+    def arriving(t):
+        return jnp.where(t < 2, x, 1 - x) * 2 + jnp.where(lax.rem(t, 2) == 0, c, 1 - c)
 
     def real_rows(j, width):
         t = lax.broadcasted_iota(jnp.int32, (BLOCK, width), 0)
@@ -759,11 +785,12 @@
     lax.fori_loop(0, 4, project, 0)
     gather_1.slivers()
     gather_2.along_z()
-    sublanes = lax.broadcasted_iota(jnp.int32, (LANES, chunk), 0)
+    half = rows // 2
+    sublanes = lax.broadcasted_iota(jnp.int32, (LANES, half), 0)
 
     def attend(step, carry):
-        head, part = lax.div(step, rows // chunk), lax.rem(step, rows // chunk)
-        at = pl.ds(pl.multiple_of(part * chunk, chunk), chunk)
+        head, part = lax.rem(step, 4), jnp.where(step < 4, 1 - x, x)
+        at = pl.ds(pl.multiple_of(part * half, LANES), half)
         scores = mm(qkv[4 + head], qkv[head, at, :], NT)
         top = jnp.max(scores, 0, keepdims=True)
         weights = jnp.exp((scores - top) * scale).astype(BF16)
@@ -775,12 +802,17 @@
         lse[head, :, at] = top * scale + jnp.log(total)
         return carry
 
-    lax.fori_loop(0, 2 * (rows // chunk), attend, 0)
+    lax.fori_loop(0, 4, attend, 0)
     gather_1.forward(1)
-    lax.fori_loop(2 * (rows // chunk), 4 * (rows // chunk), attend, 0)
+    o_finish()
+    sum_one = SeqSum(lambda j: mm(attm[token_rows(j), :], wo[...], NN), sb_a, cr_a, xr_a)
+    sum_one.run(0, 2)
+    sum_one.across()
+    lax.fori_loop(4, 8, attend, 0)
+    sum_one.run(2, 4)
     gather_1.relay()
     gather_2.slivers()
-
+    gather_1.forward(2)
     cot_in.finish()
     bias_parts = Tiles(dg, 14 * PIECE, 8, 8)
     bias_parts.fill(fc1_bias)
@@ -793,12 +825,8 @@
             mine = jnp.where(s == to, part, mine)
         fb[:, at * LANES : (at + 1) * LANES] = jnp.where(row_lanes < width, mine, 0.0)[0:1]
 
-    gather_1.forward(2)
-    o_finish()
-    sum_one = seq_sum_start(lambda j: mm(attm[token_rows(j), :], wo[...], NN), sb_a, cr_a)
-    seq_sum_across(sum_one, sb_a, cr_a, xr_a)
     gather_1.forward_far()
-    branch = seq_sum_finish(sum_one, sb_a, cr_a, xr_a)
+    branch = sum_one.finish()
     middle_rows = xs[token_rows(s), :].astype(F32) + branch + bias_out
     o_mixed[0] = middle_rows[0:slice_len]
     hat, _ = normalize(middle_rows)
@@ -806,15 +834,13 @@
     h2_in = TokenGather(h2)
     h2_in.start(h2.at[token_rows(s)])
     gather_2.forward(1)
-    h2_in.forward()
-    gather_2.forward(2)
-    gather_2.relay()
-    h2_in.finish()
     gather_1.finish()
 
     slope = (2.0 / 3.141592653589793) ** 0.5
 
-    def widen(j, carry):
+    def widen(t, carry):
+        h2_in.take_step(t)
+        j = arriving(t)
         pre = mm(h2[token_rows(j), :], w1[...], NN) + fb[...]
         square = pre * pre
         curve = jnp.tanh(slope * pre * (1.0 + 0.044715 * square))
@@ -823,7 +849,11 @@
         dg[token_rows(j), :] = half + 0.5 * slope * pre * (1.0 - curve * curve) * (1.0 + 0.134145 * square)
         return carry
 
-    lax.fori_loop(0, 4, widen, 0)
+    lax.fori_loop(0, 2, widen, 0)
+    gather_2.forward(2)
+    gather_2.relay()
+    lax.fori_loop(2, 4, widen, 0)
+    h2_in.sent()
     gather_2.forward_far()
 
     def column_products(left, right, out):
@@ -843,18 +873,18 @@
         low = (mm(gc[at, :], w2[...], NN) * dg[at, :]).astype(BF16)
         gp[at, :] = low
         column = jnp.sum(low.astype(F32), 0, keepdims=True)
-        sms[0, pl.ds(8 + s, 1), :] += column
+        sms[0, 6:7, :] += column
         return mm(low, w1[...], NT)
 
     gather_1.sent()
-    sum_two = seq_sum_start(hidden_back, sb_a, cr_a)
-    seq_sum_across(sum_two, sb_a, cr_a, xr_a)
+    sum_two = SeqSum(hidden_back, sb_a, cr_a, xr_a)
+    sum_two.run()
     reduce_2.across_last()
     column_products(h2, gp, g1)
     reduce_1.across_y()
     reduce_2.along_z(3)
     reduce_2.along_z(2)
-    grad_h = seq_sum_finish(sum_two, sb_a, cr_a, xr_a)
+    grad_h = sum_two.finish()
     hat, inverse = normalize(padded(o_mixed))
     kept = gc[token_rows(s), :].astype(F32)
     grad_x = kept + norm_back(grad_h, gain_two, hat, inverse)
@@ -868,18 +898,19 @@
     gb_in = TokenGather(gc)
     gb_in.start(gc.at[token_rows(s)])
 
-    sum_three = seq_sum_start(lambda j: mm(act[token_rows(j), :], w2[...], NT), sb_b, cr_b)
-    seq_sum_across(sum_three, sb_b, cr_b, xr_b)
+    sum_three = SeqSum(lambda j: mm(act[token_rows(j), :], w2[...], NT), sb_b, cr_b, xr_b)
+    sum_three.run()
     reduce_2.along_z(1)
     reduce_1.across_last()
-    gb_in.forward()
-    gb_in.finish()
-
-    def attended_back(j, carry):
+
+    def attended_back(t, carry):
+        gb_in.take_step(t)
+        j = arriving(t)
         attm[token_rows(j), :] = mm(gc[token_rows(j), :], wo[...], NT).astype(BF16)
         return carry
 
     lax.fori_loop(0, 4, attended_back, 0)
+    gb_in.sent()
 
     o_sent()
 
@@ -891,8 +922,6 @@
     lax.fori_loop(0, 4, out_products, 0)
     ro_across_y()
     reduce_2.relay()
-    branch = seq_sum_finish(sum_three, sb_b, cr_b, xr_b)
-    o_mixed[0] = jnp.where(real_rows(s, d), padded(o_mixed) + branch + bias_two, 0.0)[0:slice_len]
 
     wide_lanes = lane_ids(rows)
     chunk_lanes = lane_ids(chunk)
@@ -930,6 +959,8 @@
     reduce_1.along_z(1)
     reduce_1.relay()
 
+    branch = sum_three.finish()
+    o_mixed[0] = jnp.where(real_rows(s, d), padded(o_mixed) + branch + bias_two, 0.0)[0:slice_len]
     gpj = h2.at[:, 0:qw]
 
     def pack(j, carry):
@@ -939,10 +970,6 @@
         return carry
 
     lax.fori_loop(0, 4, pack, 0)
-    column_products(h1, gpj, gq)
-    reduce_q.across_y()
-    ro_along_z()
-    reduce_2.pieces()
 
     def tokens_back(j):
         part = mm(gpj[token_rows(j), :], wq[...], NT)
@@ -951,7 +978,8 @@
         sms[0, 2:3, :] += jnp.sum(part, 0, keepdims=True)
         return part
 
-    sum_four = seq_sum_start(tokens_back, sb_a, cr_a)
+    sum_four = SeqSum(tokens_back, sb_a, cr_a, xr_a)
+    sum_four.run()
     sm_at, sh_at = take(7), take(7)
 
     def vectors(stage, slots, devices):
@@ -971,26 +999,32 @@
 
     z_to_all, z_from_all = [z_dev(t) for t in (1, 2, 3)], [z_dev(-t) for t in (1, 2, 3)]
     s_to_all, s_from_all = [(i, s_at(t)) for t in (1, 2, 3)], [(i, s_at(-t)) for t in (1, 2, 3)]
-    vectors(0, (1, 2, 3), z_to_all)
-    seq_sum_across(sum_four, sb_a, cr_a, xr_a)
+    vectors(0, (0,), (y_peer,))
+    column_products(h1, gpj, gq)
+    reduce_q.across_y()
+    sms[1], shs[1] = vectors_sum(0, (0,), (y_peer,))
+    vectors(1, (1, 2, 3), z_to_all)
+    ro_along_z()
+    reduce_2.pieces()
     reduce_q.along_z(3, 2)
     reduce_q.relay()
-    grad_h = seq_sum_finish(sum_four, sb_a, cr_a, xr_a)
+    grad_h = sum_four.finish()
     hat, inverse = normalize(xs[token_rows(s), :].astype(F32))
     o_gtok[0] = (padded(o_gtok) + norm_back(grad_h, gain_one, hat, inverse))[0:slice_len]
     reduce_q.along_z(1)
-    sms[1], shs[1] = vectors_sum(0, (1, 2, 3), z_from_all)
-    vectors(1, (4, 5, 6), s_to_all)
+    sms[2], shs[2] = vectors_sum(1, (1, 2, 3), z_from_all)
+    vectors(2, (4, 5, 6), s_to_all)
     reduce_1.pieces()
     reduce_2.finish()
     reduce_2.publish_wide(o_2)
-    sms[2], shs[2] = vectors_sum(1, (4, 5, 6), s_from_all)
-    vectors(2, (0,), (y_peer,))
     ro_pieces()
     reduce_q.pieces()
     reduce_1.finish()
     reduce_1.publish_wide(o_1)
-    summed_rows, by_head = vectors_sum(2, (0,), (y_peer,))
+    summed_rows, by_head = vectors_sum(2, (4, 5, 6), s_from_all)
+    prm[pl.ds(s, 1), :] = sms[2, 6:7, :]
+    for t in (1, 2, 3):
+        prm[pl.ds(s_at(-t), 1), :] = smr[3 + t, 6:7, :]
     mine = smr.at[1]
     for to, row in enumerate((0, 1, 2, None, None, 3, 4, 5)):
         if row is not None:
@@ -1007,7 +1041,7 @@
     for j in range(4):
         tile, offset = divmod(j * f, LANES)
         for t in range(w1.shape[1] // LANES):
-            part = summed_rows[8 + j : 9 + j, t * LANES : (t + 1) * LANES]
+            part = prm[j : j + 1, t * LANES : (t + 1) * LANES]
             if offset:
                 part = pltpu.roll(part, offset, 1)
             for to, where in ((tile + t, one_lane >= offset), (tile + t + 1, one_lane < offset)):
@@ -1088,8 +1122,8 @@
         pltpu.VMEM((1, f_pad), F32),
         pltpu.VMEM((8, d), F32),
         pltpu.VMEM((2, 16, LANES), F32),
-        pltpu.VMEM((3, 16, d), F32),
-        pltpu.VMEM((7, 16, d), F32),
+        pltpu.VMEM((3, 8, d), F32),
+        pltpu.VMEM((7, 8, d), F32),
         pltpu.VMEM((3, 32, LANES), F32),
         pltpu.VMEM((7, 32, LANES), F32),
         pltpu.SemaphoreType.DMA((200,)),

time: 222 us -> 217 us (0.977)
  Pallas kernels: 216 us -> 213 us
    pallas_call x1, Pallas kernels: 212 us -> 209 us  [whole_layer(): pl.pallas_call(partial(layer_kernel, (slice_len, d, hd, f, qw, n_z)), out...]
where the time goes in v5:
time: 217 us
  Pallas kernels  213 us (98%)
    pallas_call x1, Pallas kernels, whole_layer(): pl.pallas_call(partial(layer_kernel, (slice_len, d, hd, f, qw, n_z)), out...  209 us

profile of v5, /device:TPU:1, one launch (start us, length us, event | category | flops | bytes accessed | tf_op | source)
XLA Modules:
  0.0 216.9 jit_solution(16158165556759008217)
XLA Ops:
  0.6 1.3 broadcast_in_dim.3.fc1_bias
  2.6 208.9 %shard_map.169 = (f32[1,183,1152]{2,1,0:T(8,128)}, f32[1,183,1152]{2,1,0:T(8,128)}, f32[36,3456]{1,0:T(8,128)}, bf16[48,1152]{1,0:T(8,128)(2,1)}, f32[36,4304]{1...) custom-call(s32[1]{0:T(128)S(6)} %copy.19.off_ref, ...), custom_call_target="tpu_custom_call" | custom-call | tf_op jit(solution)/shard_map/pallas_call | solution.py:1133
  211.5 4.0 %shard_map.170 = (f32[183,1,1152]{2,1,0:T(1,128)}, f32[183,1,1152]{2,1,0:T(1,128)}, f32[36,3456]{1,0:T(8,128)}, f32[36,4304]{1,0:T(8,128)}, f32[36,4304]{1,0:T(8...) custom-call(f32[1,183,1152]{2,1,0:T(8,128)} %get-tuple-element.26.mixed, ...), custom_call_target="tpu_custom_call" | custom-call | tf_op jit(solution)/shard_map/pallas_call | solution.py:1147
  215.5 0.0 copy-start
  215.5 0.7 copy-done
  216.2 0.7 reduce
Async XLA Ops:
  215.5 0.7 copy-start

commit v6 on v5

--- a/solution.py
+++ b/solution.py
@@ -200,6 +200,12 @@
     def token_rows(j):
         return pl.ds(pl.multiple_of(j * BLOCK, BLOCK), BLOCK)
 
+    half_block = BLOCK // 2
+    halves = (slice(0, half_block), slice(half_block, BLOCK))
+
+    def half_rows(j, p):
+        return pl.ds(pl.multiple_of(j * BLOCK + p * half_block, 32), half_block)
+
     def img_rows(b):
         return pl.ds(pl.multiple_of(b * rb, 16), rb)
 
@@ -393,55 +399,58 @@
     class TokenGather:
         def __init__(self, full):
             self.full = full
-            self.sx, self.sc, self.sd = take(), take(), take()
-
-        def at(self, j):
-            return self.full.at[token_rows(j)]
-
-        def start(self, own):
-            self.own = own
-            copy(own, self.at(s), self.sx, x_peer).start()
-            copy(own, self.at(s), self.sc, core_peer).start()
+            self.sx, self.sc, self.sd = take(2), take(2), take(2)
+
+        def hop(self, j, p, index, device):
+            rows_p = self.full.at[half_rows(j, p)]
+            return copy(rows_p, rows_p, index + p, device)
+
+        def start(self, *halves):
+            for p in halves:
+                self.hop(s, p, self.sx, x_peer).start()
+                self.hop(s, p, self.sc, core_peer).start()
 
         def forward(self):
-            across = self.at((1 - x) * 2 + c)
-            copy(across, across, self.sx, x_peer).wait_recv()
-            copy(across, across, self.sd, core_peer).start()
+            for p in (0, 1):
+                made = self.hop((1 - x) * 2 + c, p, self.sx, x_peer)
+                made.wait_recv()
+                self.hop((1 - x) * 2 + c, p, self.sd, core_peer).start()
+
+        def wait_core(self):
+            for p in (0, 1):
+                self.hop(x * 2 + 1 - c, p, self.sc, core_peer).wait_recv()
+
+        def wait_last(self):
+            for p in (0, 1):
+                self.hop((1 - x) * 2 + 1 - c, p, self.sd, core_peer).wait_recv()
 
         def take_step(self, t):
-            @pl.when(t == 1)
-            def _():
-                came = self.at(x * 2 + 1 - c)
-                copy(came, came, self.sc, core_peer).wait_recv()
-
+            pl.when(t == 1)(self.wait_core)
             pl.when(t == 2)(self.forward)
-
-            @pl.when(t == 3)
-            def _():
-                came = self.at((1 - x) * 2 + 1 - c)
-                copy(came, came, self.sd, core_peer).wait_recv()
+            pl.when(t == 3)(self.wait_last)
 
         def sent(self):
-            copy(self.own, self.at(s), self.sx, x_peer).wait_send()
-            copy(self.own, self.at(s), self.sc, core_peer).wait_send()
-            across = self.at((1 - x) * 2 + c)
-            copy(across, across, self.sd, core_peer).wait_send()
+            for p in (0, 1):
+                self.hop(s, p, self.sx, x_peer).wait_send()
+                self.hop(s, p, self.sc, core_peer).wait_send()
+                self.hop((1 - x) * 2 + c, p, self.sd, core_peer).wait_send()
 
         def finish(self):
-            for index, j in ((self.sc, x * 2 + 1 - c), (self.sd, (1 - x) * 2 + 1 - c)):
-                copy(self.at(j), self.at(j), index, core_peer).wait_recv()
+            self.wait_core()
+            self.wait_last()
             self.sent()
 
     class SeqSum:
         def __init__(self, partial, sb, cr, xr):
             self.partial, self.sb, self.cr, self.xr = partial, sb, cr, xr
-            self.first, self.last = take(2), take()
+            self.first, self.last = take(2), take(2)
 
         def to_core(self, slot):
             return copy(self.sb.at[slot], self.cr.at[slot], self.first + slot, core_peer)
 
-        def to_chip(self):
-            return copy(self.sb.at[2], self.xr, self.last, x_peer)
+        def to_chip(self, p):
+            own_half = pl.ds(p * half_block, half_block)
+            return copy(self.sb.at[2, own_half], self.xr.at[own_half], self.last + p, x_peer)
 
         def run(self, low=0, high=4):
             partial = self.partial
@@ -467,16 +476,18 @@
 
         def across(self):
             copy(self.cr.at[0], self.cr.at[0], self.first, core_peer).wait_recv()
-            self.sb[2] = (pf[0] + self.cr[0].astype(F32)).astype(BF16)
-            self.to_chip().start()
-
-        def finish(self):
-            copy(self.cr.at[1], self.cr.at[1], self.first + 1, core_peer).wait_recv()
-            copy(self.xr, self.xr, self.last, x_peer).wait_recv()
-            for slot in range(2):
-                self.to_core(slot).wait_send()
-            self.to_chip().wait_send()
-            return pf[1] + self.cr[1].astype(F32) + self.xr[...].astype(F32)
+            for p, at in enumerate(halves):
+                self.sb[2, at, :] = (pf[0, at, :] + self.cr[0, at, :].astype(F32)).astype(BF16)
+                self.to_chip(p).start()
+
+        def finish(self, p):
+            at = halves[p]
+            if p == 0:
+                copy(self.cr.at[1], self.cr.at[1], self.first + 1, core_peer).wait_recv()
+            self.to_chip(p).wait_recv()
+            self.to_chip(p).wait_send()
+            self.to_core(p).wait_send()
+            return pf[1, at, :] + self.cr[1, at, :].astype(F32) + self.xr[at, :].astype(F32)
 
     class Reduce:
         def __init__(self, grad, yr, zr, zs, fs, out):
@@ -673,10 +684,18 @@
         position = j * slice_len + t
         return (t < slice_len) & (position >= off_ref[0]) & (position < off_ref[0] + VALID)
 
-    def padded(rows_in):
+    def half_of(rows_in, p):
+        if p == 0:
+            return rows_in[0, halves[0], :]
         pf[0, BLOCK - 16 : BLOCK, :] = jnp.zeros((16, d), F32)
-        pf[0, 0:slice_len, :] = rows_in[0]
-        return pf[0]
+        pf[0, half_block:slice_len, :] = rows_in[0, half_block:slice_len, :]
+        return pf[0, halves[1], :]
+
+    def put_half(rows_out, p, value):
+        if p == 0:
+            rows_out[0, halves[0], :] = value
+        else:
+            rows_out[0, half_block:slice_len, :] = value[0 : slice_len - half_block]
 
     tokens_in, cot_in = TokenGather(xs), TokenGather(gc)
     piece_lanes = lane_ids(PIECE)
@@ -704,7 +723,7 @@
     pf[0, BLOCK - 16 : BLOCK, :] = jnp.zeros((16, d), F32)
     pf[0, 0:slice_len, :] = tok[0].astype(F32)
     xs[token_rows(s), :] = pf[0].astype(BF16)
-    tokens_in.start(xs.at[token_rows(s)])
+    tokens_in.start(0, 1)
     out_rows = Tiles(dg, 12 * PIECE, PIECE, PIECE)
     out_rows.fill(w_out)
     for at in range(d // LANES):
@@ -725,7 +744,7 @@
     pf[1, BLOCK - 16 : BLOCK, :] = jnp.zeros((16, d), F32)
     pf[1, 0:slice_len, :] = cot[0].astype(F32)
     gc[token_rows(s), :] = jnp.where(real_rows(s, d), pf[1], 0.0).astype(BF16)
-    cot_in.start(gc.at[token_rows(s)])
+    cot_in.start(0, 1)
     sms[0] = jnp.zeros(sms.shape[1:], F32)
     shs[0] = jnp.zeros(shs.shape[1:], F32)
     tmp[...] = jnp.zeros(tmp.shape, F32)
@@ -815,7 +834,7 @@
     gather_1.forward(2)
     cot_in.finish()
     bias_parts = Tiles(dg, 14 * PIECE, 8, 8)
-    bias_parts.fill(fc1_bias)
+    bias_parts.fill(fc1_bias[...].astype(F32)[None])
     row_lanes = lane_ids(8)
     for at in range(w1.shape[1] // LANES):
         width = min(LANES, f - at * LANES)
@@ -826,13 +845,13 @@
         fb[:, at * LANES : (at + 1) * LANES] = jnp.where(row_lanes < width, mine, 0.0)[0:1]
 
     gather_1.forward_far()
-    branch = sum_one.finish()
-    middle_rows = xs[token_rows(s), :].astype(F32) + branch + bias_out
-    o_mixed[0] = middle_rows[0:slice_len]
-    hat, _ = normalize(middle_rows)
-    h2[token_rows(s), :] = (hat * gain_two + shift_two).astype(BF16)
     h2_in = TokenGather(h2)
-    h2_in.start(h2.at[token_rows(s)])
+    for p in (0, 1):
+        middle_rows = xs[half_rows(s, p), :].astype(F32) + sum_one.finish(p) + bias_out
+        put_half(o_mixed, p, middle_rows)
+        hat, _ = normalize(middle_rows)
+        h2[half_rows(s, p), :] = (hat * gain_two + shift_two).astype(BF16)
+        h2_in.start(p)
     gather_2.forward(1)
     gather_1.finish()
 
@@ -884,19 +903,18 @@
     reduce_1.across_y()
     reduce_2.along_z(3)
     reduce_2.along_z(2)
-    grad_h = sum_two.finish()
-    hat, inverse = normalize(padded(o_mixed))
-    kept = gc[token_rows(s), :].astype(F32)
-    grad_x = kept + norm_back(grad_h, gain_two, hat, inverse)
-    o_gtok[0] = grad_x[0:slice_len]
-    low = grad_x.astype(BF16)
-    sms[0, 1:2, :] = jnp.sum(grad_h * hat, 0, keepdims=True)
-    sms[0, 4:5, :] = jnp.sum(grad_h, 0, keepdims=True)
-    sms[0, 5:6, :] = jnp.sum(kept, 0, keepdims=True)
-    sms[0, 3:4, :] = jnp.sum(low.astype(F32), 0, keepdims=True)
-    gc[token_rows(s), :] = low
     gb_in = TokenGather(gc)
-    gb_in.start(gc.at[token_rows(s)])
+    for p in (0, 1):
+        grad_h = sum_two.finish(p)
+        hat, inverse = normalize(half_of(o_mixed, p))
+        kept = gc[half_rows(s, p), :].astype(F32)
+        grad_x = kept + norm_back(grad_h, gain_two, hat, inverse)
+        put_half(o_gtok, p, grad_x)
+        low = grad_x.astype(BF16)
+        gc[half_rows(s, p), :] = low
+        gb_in.start(p)
+        for row, column in ((1, grad_h * hat), (4, grad_h), (5, kept), (3, low.astype(F32))):
+            sms[0, row : row + 1, :] += jnp.sum(column, 0, keepdims=True)
 
     sum_three = SeqSum(lambda j: mm(act[token_rows(j), :], w2[...], NT), sb_b, cr_b, xr_b)
     sum_three.run()
@@ -959,8 +977,9 @@
     reduce_1.along_z(1)
     reduce_1.relay()
 
-    branch = sum_three.finish()
-    o_mixed[0] = jnp.where(real_rows(s, d), padded(o_mixed) + branch + bias_two, 0.0)[0:slice_len]
+    for p, at in enumerate(halves):
+        total = half_of(o_mixed, p) + sum_three.finish(p) + bias_two
+        put_half(o_mixed, p, jnp.where(real_rows(s, d)[at], total, 0.0))
     gpj = h2.at[:, 0:qw]
 
     def pack(j, carry):
@@ -1008,9 +1027,10 @@
     reduce_2.pieces()
     reduce_q.along_z(3, 2)
     reduce_q.relay()
-    grad_h = sum_four.finish()
-    hat, inverse = normalize(xs[token_rows(s), :].astype(F32))
-    o_gtok[0] = (padded(o_gtok) + norm_back(grad_h, gain_one, hat, inverse))[0:slice_len]
+    for p in (0, 1):
+        grad_h = sum_four.finish(p)
+        hat, inverse = normalize(xs[half_rows(s, p), :].astype(F32))
+        put_half(o_gtok, p, half_of(o_gtok, p) + norm_back(grad_h, gain_one, hat, inverse))
     reduce_q.along_z(1)
     sms[2], shs[2] = vectors_sum(1, (1, 2, 3), z_from_all)
     vectors(2, (4, 5, 6), s_to_all)
@@ -1060,8 +1080,8 @@
         made.wait_send()
 
 
-def hand_over(mixed, tokens, g_qkv, g_1, g_2, g_out, g_gains, g_biases, *outs):
-    o_mixed, o_tokens, o_qkv, o_1, o_2, o_out, o_gains, o_biases = outs
+def hand_over(mixed, tokens, g_qkv, g_1, g_2, g_out, g_gains, g_biases, g_fb, *outs):
+    o_mixed, o_tokens, o_qkv, o_1, o_2, o_out, o_gains, o_biases, o_fb = outs
     o_qkv[...] = g_qkv[...]
     o_1[...] = g_1[...]
     o_2[...] = g_2[...]
@@ -1070,6 +1090,7 @@
     o_out[...] = g_out[0 : o_out.shape[0], :].astype(F32)
     o_gains[...] = g_gains[...]
     o_biases[...] = g_biases[...]
+    o_fb[...] = g_fb[0]
 
 
 def whole_layer(tokens, offsets, w_qkv, w_out, w_fc1, w_fc2, gains, biases, fc1_bias, cotangent):
@@ -1139,19 +1160,19 @@
         compiler_params=pltpu.CompilerParams(
             collective_id=0, has_side_effects=True, vmem_limit_bytes=VMEM_BYTES
         ),
-    )(offsets, w_qkv, w_out, w_fc1, w_fc2, gains.T, biases.T, fc1_bias[None], tokens, cotangent)
+    )(offsets, w_qkv, w_out, w_fc1, w_fc2, gains.T, biases.T, fc1_bias, tokens, cotangent)
 
     rows_out = jax.ShapeDtypeStruct((slice_len, 1, d), F32)
     same = [jax.ShapeDtypeStruct(made.shape, F32) for made in (gq, g1, g2)]
-    rest = [jax.ShapeDtypeStruct(shape, F32) for shape in ((own, d), (2, own), (6, own))]
-    mixed, grad_tokens, gq, g1, g2, go, g_gains, g_biases = pl.pallas_call(
+    rest = [jax.ShapeDtypeStruct(shape, F32) for shape in ((own, d), (2, own), (6, own), (wide,))]
+    mixed, grad_tokens, gq, g1, g2, go, g_gains, g_biases, g_fb = pl.pallas_call(
         hand_over,
         out_shape=[rows_out, rows_out, *same, *rest],
-        in_specs=[vmem] * 8,
-        out_specs=[vmem] * 8,
-    )(mixed, grad_tokens, gq, g1, g2, go, g_gains, g_biases)
+        in_specs=[vmem] * 9,
+        out_specs=[vmem] * 9,
+    )(mixed, grad_tokens, gq, g1, g2, go, g_gains, g_biases, g_fb)
     mixed, grad_tokens = mixed.reshape(tokens.shape), grad_tokens.reshape(tokens.shape)
-    return mixed, grad_tokens, gq, go, g1, g2, g_gains.T, g_biases.T, g_fb.reshape(wide)
+    return mixed, grad_tokens, gq, go, g1, g2, g_gains.T, g_biases.T, g_fb
 
 
 def local(tokens, offsets, w_qkv, w_out, w_fc1, w_fc2, gains, biases, fc1_bias, cotangent):

time: 217 us -> 215 us (level)
  no operation moved by 1% of the time
where the time goes in v6:
time: 215 us; the launch traced here: 214 us
  Pallas kernels  213 us (99%)
    pallas_call x1, Pallas kernels, whole_layer(): pl.pallas_call(partial(layer_kernel, (slice_len, d, hd, f, qw, n_z)), out...  209 us

profile of v6, /device:TPU:1, one launch (start us, length us, event | category | flops | bytes accessed | tf_op | source)
XLA Modules:
  0.0 214.4 jit_solution(15462624857975419736)
XLA Ops:
  1.3 209.0 %shard_map.169 = (f32[1,183,1152]{2,1,0:T(8,128)}, f32[1,183,1152]{2,1,0:T(8,128)}, f32[36,3456]{1,0:T(8,128)}, bf16[48,1152]{1,0:T(8,128)(2,1)}, f32[36,4304]{1...) custom-call(s32[1]{0:T(128)S(6)} %copy.19.off_ref, ...), custom_call_target="tpu_custom_call" | custom-call | tf_op jit(solution)/shard_map/pallas_call | solution.py:1154
  210.3 4.0 %shard_map.170 = (f32[183,1,1152]{2,1,0:T(1,128)}, f32[183,1,1152]{2,1,0:T(1,128)}, f32[36,3456]{1,0:T(8,128)}, f32[36,4304]{1,0:T(8,128)}, f32[36,4304]{1,0:T(8...) custom-call(f32[1,183,1152]{2,1,0:T(8,128)} %get-tuple-element.27.mixed, ...), custom_call_target="tpu_custom_call" | custom-call | tf_op jit(solution)/shard_map/pallas_call | solution.py:1168

commit v7 on v6

--- a/solution.py
+++ b/solution.py
@@ -729,7 +729,7 @@
     for at in range(d // LANES):
         yo[0, 0:PIECE, at * LANES : (at + 1) * LANES] = out_rows[at].astype(BF16)
     o_start()
-    for weights, first, pieces in ((w_fc1, 4, y1), (w_fc2, 8, y2)):
+    def cut_wide(weights, first, pieces, gather):
         wide = Tiles(dg, first * PIECE, PIECE, PIECE)
         wide.fill(weights)
         for to in range(4):
@@ -740,11 +740,8 @@
                 if width < LANES:
                     part = jnp.where(piece_lanes < width, part, 0.0)
                 pieces[to, 0:PIECE, at * LANES : (at + 1) * LANES] = part.astype(BF16)
-        (gather_1 if first == 4 else gather_2).pieces()
-    pf[1, BLOCK - 16 : BLOCK, :] = jnp.zeros((16, d), F32)
-    pf[1, 0:slice_len, :] = cot[0].astype(F32)
-    gc[token_rows(s), :] = jnp.where(real_rows(s, d), pf[1], 0.0).astype(BF16)
-    cot_in.start(0, 1)
+        gather.pieces()
+
     sms[0] = jnp.zeros(sms.shape[1:], F32)
     shs[0] = jnp.zeros(shs.shape[1:], F32)
     tmp[...] = jnp.zeros(tmp.shape, F32)
@@ -754,8 +751,14 @@
     gather_q.across_y()
     o_assemble()
     o_along_z()
+    cut_wide(w_fc1, 4, y1, gather_1)
     gather_q.forward(1)
     tokens_in.forward()
+    cut_wide(w_fc2, 8, y2, gather_2)
+    pf[1, BLOCK - 16 : BLOCK, :] = jnp.zeros((16, d), F32)
+    pf[1, 0:slice_len, :] = cot[0].astype(F32)
+    gc[token_rows(s), :] = jnp.where(real_rows(s, d), pf[1], 0.0).astype(BF16)
+    cot_in.start(0, 1)
     gather_1.assemble()
     gather_q.slivers()
     gather_q.forward(2)

time: 215 us -> 215 us (level)
  no operation moved by 1% of the time
where the time goes in v7:
time: 215 us; the launch traced here: 214 us
  Pallas kernels  213 us (99%)
    pallas_call x1, Pallas kernels, whole_layer(): pl.pallas_call(partial(layer_kernel, (slice_len, d, hd, f, qw, n_z)), out...  209 us

profile of v7, /device:TPU:1, one launch (start us, length us, event | category | flops | bytes accessed | tf_op | source)
XLA Modules:
  0.0 214.4 jit_solution(10477797200505101283)
XLA Ops:
  1.3 209.0 %shard_map.169 = (f32[1,183,1152]{2,1,0:T(8,128)}, f32[1,183,1152]{2,1,0:T(8,128)}, f32[36,3456]{1,0:T(8,128)}, bf16[48,1152]{1,0:T(8,128)(2,1)}, f32[36,4304]{1...) custom-call(s32[1]{0:T(128)S(6)} %copy.19.off_ref, ...), custom_call_target="tpu_custom_call" | custom-call | tf_op jit(solution)/shard_map/pallas_call | solution.py:1157
  210.3 4.0 %shard_map.170 = (f32[183,1,1152]{2,1,0:T(1,128)}, f32[183,1,1152]{2,1,0:T(1,128)}, f32[36,3456]{1,0:T(8,128)}, f32[36,4304]{1,0:T(8,128)}, f32[36,4304]{1,0:T(8...) custom-call(f32[1,183,1152]{2,1,0:T(8,128)} %get-tuple-element.27.mixed, ...), custom_call_target="tpu_custom_call" | custom-call | tf_op jit(solution)/shard_map/pallas_call | solution.py:1171
